TPU v7x, 32 devices: a whole 2x2x4 slice. The times are simulated.
32 devices in a mesh: grp: 2 (over y), tchunk: 2 (over x), ha: 4 (over z), wa: 2 (over core).
Axes of the slice: x: 2, y: 2, z: 4, core: 2. Of those that a mesh axis runs over, the one named last changes fastest.
Arguments:
- features: bfloat16 [32, 32, 16, 192], P(('grp', 'tchunk'), 'ha', 'wa'), parts along dimension 0, may hold values from -6 to 6
- frame_counts: int32 [4], P(('grp', 'tchunk')), parts along dimension 0, may hold values from 0 to 8, as said below
- gain_first: float32 [192], replicated, may hold values from 0.25 to 1.75
- conv_first: bfloat16 [3, 3, 3, 192, 192], replicated, may hold values from -0.078125 to 0.078125
- bias_first: float32 [192], replicated, may hold values from -1.8 to 1.8
- gain_second: float32 [192], replicated, may hold values from 0.25 to 1.75
- conv_second: bfloat16 [3, 3, 3, 192, 192], replicated, may hold values from -0.078125 to 0.078125
- bias_second: float32 [192], replicated, may hold values from -1.8 to 1.8
Outputs:
- decoded: bfloat16 [32, 32, 16, 192], P(('grp', 'tchunk'), 'ha', 'wa'), parts along dimension 0
There are 2 independent parts, one for each index of `grp`. A program takes and returns all parts, laid end to end along the dimension named above; an argument that names none is the same for every part. Nothing has to cross between parts.
Inputs may be any that keep to these rules, and one draw needn't show every extreme that they name: `frame_counts`: in every draw some temporal block has all 8 slots live; any block may have none.
All inputs are finite; a program needn't handle non-finite values.
Results may differ from a plain program's by a relative error of at most 0.0039.
Values may be sent and summed in bfloat16 or wider, within the bound.
No kernel may reach another device: no remote copies, remote signals or barrier semaphores. Data moves between devices by JAX's collectives and lax.ppermute only.
A program may use at most 64 MiB of HBM per device.

v0:
```python
import jax
import jax.numpy as jnp
from jax import lax
from jax.experimental import pallas as pl
from jax.experimental.pallas import tpu as pltpu
from jax.sharding import PartitionSpec as P

epsilon = 1e-06
CACHE = 4
TAPS = 3
LANES = 128
PRODUCT = 64


def slots_kernel(slots_ref):
    slots_ref[...] = lax.broadcasted_iota(jnp.int32, slots_ref.shape, 0)


def prepare_kernel(total_ref, slots_ref, raw, tail_ref, mine_ref, theirs_ref, marks_ref, pack):
    frames, rows = raw.shape[:2]
    pairs, held = rows // 2, mine_ref.shape[1]
    core = lax.axis_index("wa")
    total = total_ref[0]
    for frame in range(frames):
        for pair in range(pairs):
            first, second = raw[frame, 2 * pair], raw[frame, 2 * pair + 1]
            packed = jnp.concatenate(
                [first[:, :LANES], second[:, :LANES], first[:, LANES:], second[:, LANES:]], axis=-1
            )
            pack[frame, pair] = packed
    for place, ref in ((core, tail_ref), (1 - core, theirs_ref)):
        for slot in range(CACHE):
            frame = total - CACHE + slot
            value = pack[jnp.maximum(frame, 0), pl.ds(place * (pairs - held), held)]
            ref[slot * held:(slot + 1) * held] = jnp.where(frame >= 0, value, jnp.zeros_like(value))
    for frame in range(frames):
        start = (CACHE + frame) * held
        value = pack[frame, pl.ds(core * (pairs - held), held)]
        mine_ref[frame] = jnp.where(frame < total, value, jnp.zeros_like(value))
        value = pack[frame, pl.ds((1 - core) * (pairs - held), held)]
        theirs_ref[start:start + held] = jnp.where(frame < total, value, jnp.zeros_like(value))
    slot = slots_ref[...]
    tail_ref[CACHE * held] = jnp.where(
        (slot < CACHE) & (total - CACHE + slot >= 0), 1.0, 0.0
    ).astype(tail_ref.dtype)
    marks_ref[...] = jnp.where(slot < total, 1.0, 0.0).astype(marks_ref.dtype)


def joined_tails(mine, other):
    count = lax.axis_size("tchunk")
    if count <= 2:
        return mine, other
    tiles = other.shape[0]
    value = jnp.concatenate([mine, other], axis=0)

    def apart(value):
        return jnp.concatenate([
            value[:tiles].reshape((CACHE, -1) + value.shape[1:]),
            value[tiles + 1:].reshape((CACHE, -1) + value.shape[1:]),
        ], axis=1), value[tiles, :CACHE]

    def pushed(value, held):
        return lax.dynamic_slice_in_dim(jnp.concatenate([value, jnp.zeros_like(value)], axis=0), held, CACHE, 0)

    step = 1
    while step < count - 1:
        early = lax.ppermute(value, "tchunk", [(k, k + step) for k in range(count - step)])
        held = jnp.sum(value[tiles, :CACHE, 0].astype(jnp.int32))
        body, marks = apart(early)
        body, marks = pushed(body, held), pushed(marks, held)
        half = body.shape[1] // 2
        marks = jnp.pad(marks, ((0, value.shape[1] - CACHE), (0, 0)))[None]
        shape = (tiles,) + value.shape[1:]
        value = value + jnp.concatenate([body[:, :half].reshape(shape), marks, body[:, half:].reshape(shape)], axis=0)
        step *= 2
    return value[:tiles + 1], value[tiles + 1:]


def silu(half):
    return half + half * jnp.tanh(half)


def lane_mask():
    return lax.broadcasted_iota(jnp.int32, (1, 1, 1, LANES), 3) < LANES // 2


def gains(gain_ref):
    low, high = 0.5 * gain_ref[:, :LANES], 0.5 * gain_ref[:, LANES:]
    return low.reshape(1, 1, 1, LANES), jnp.concatenate([high, high], axis=-1).reshape(1, 1, 1, LANES)


def rolled(values):
    shape = values.shape
    return pltpu.roll(values.reshape(-1, LANES), LANES // 2, 1).reshape(shape)


def first_rows(left, right, gain_ref, channels):
    raw = jnp.concatenate([left.astype(jnp.float32), right.astype(jnp.float32)], axis=2)
    front, back, high = raw[..., :LANES], raw[..., LANES:2 * LANES], raw[..., 2 * LANES:]
    lower = lane_mask()
    squared = high * high

    def inverse(low, mask):
        total = jnp.sum(low * low + jnp.where(mask, squared, 0.0), axis=-1, keepdims=True)
        return lax.rsqrt(total * (1.0 / channels) + epsilon)

    scale_front, scale_back = inverse(front, lower), inverse(back, jnp.logical_not(lower))
    gain_low, gain_high = gains(gain_ref)
    front = silu(front * scale_front * gain_low)
    back = silu(back * scale_back * gain_low)
    high = silu(high * jnp.where(lower, scale_front, scale_back) * gain_high)
    turned = rolled(high)
    one = [front, jnp.where(lower, high, 0.0), jnp.where(lower, 0.0, turned)]
    two = [back, jnp.where(lower, turned, 0.0), jnp.where(lower, 0.0, high)]
    return [jnp.concatenate([part.astype(jnp.bfloat16) for part in row], axis=-1) for row in (one, two)]


def second_rows(hidden, flag, gain_ref, channels):
    gain = 0.5 * gain_ref[...].reshape(1, 1, 1, channels)
    total = jnp.sum(hidden * hidden, axis=-1, keepdims=True)
    inverse = lax.rsqrt(total * (1.0 / channels) + epsilon) * flag
    values = silu(hidden * inverse * gain)
    rest = jnp.zeros(values.shape[:-1] + (LANES // 2,), jnp.float32)
    high = jnp.concatenate([values[..., LANES:], rest], axis=-1)
    parts = [values[..., :LANES], high, rolled(high)]
    return jnp.concatenate([part.astype(jnp.bfloat16) for part in parts], axis=-1)


def convolved(operand, weights_ref, bias_ref, frame, frames, rows, then):
    step = max(1, PRODUCT // (rows * operand.shape[2]))
    for start in range(0, frames, step):
        count = min(step, frames - start)
        then(start, count, convolved_part(operand, weights_ref, bias_ref, frame + start, count, rows))


def convolved_part(operand, weights_ref, bias_ref, frame, frames, rows):
    width = operand.shape[2]
    channels = weights_ref.shape[-1]
    taps = [(a, i) for a in range(TAPS) for i in range(TAPS)]
    groups = [taps[start:start + 2] for start in range(0, len(taps), 2)]

    def window(tap, part):
        a, i = tap
        value = operand[frame + a:frame + a + frames, i:i + rows, :, part * LANES:(part + 1) * LANES]
        return value.reshape(frames * rows * width, LANES)

    pieces = []
    for group in groups:
        pieces += [window(tap, 0) for tap in group]
        high = window(group[0], 1)
        pieces.append(high + window(group[1], 2) if len(group) > 1 else high)
    left = jnp.concatenate(pieces, axis=-1)
    products = []
    for j in range(TAPS):
        rights = []
        for group in groups:
            held = [weights_ref[a, i, j] for a, i in group]
            rights += [weight[:LANES] for weight in held] + [weight[LANES:] for weight in held]
        rights.append(jnp.zeros((left.shape[1] - sum(r.shape[0] for r in rights), channels), jnp.bfloat16))
        product = jnp.dot(left, jnp.concatenate(rights, axis=0), preferred_element_type=jnp.float32)
        products.append(product.reshape(frames * rows, width, channels))
    column = lax.broadcasted_iota(jnp.int32, (1, width, 1), 1)
    before = jnp.where(column == 0, 0.0, pltpu.roll(products[0], 1, 1))
    after = jnp.where(column == width - 1, 0.0, pltpu.roll(products[2], width - 1, 1))
    result = products[1] + before + after + bias_ref[...].reshape(1, 1, channels)
    return result.reshape(frames, rows, width, channels)


def halves(core, mine, other):
    return jnp.where(core == 0, mine, other), jnp.where(core == 0, other, mine)


def frame_flags(marks, frames):
    values = marks.astype(jnp.float32)
    return [values[k:k + 1, 0:1].reshape(1, 1, 1, 1) for k in frames]


def fill_rows(operand, frame, mine, other, gain_ref, channels):
    left, right = halves(lax.axis_index("wa"), mine, other)
    frames, pairs = mine.shape[:2]
    upper, lower = first_rows(left, right, gain_ref, channels)
    for pair in range(pairs):
        operand[frame:frame + frames, 2 * pair] = upper[:, pair]
        operand[frame:frame + frames, 2 * pair + 1] = lower[:, pair]


def border_kernel(tail_ref, mine_ref, other_ref, tail_edge_ref, own_edge_ref):
    frames, held = mine_ref.shape[:2]
    pair = lax.axis_index("wa") * (held - 1)
    for slot in range(CACHE):
        tail_edge_ref[0, slot] = tail_ref[slot * held + pair]
        tail_edge_ref[1, slot] = other_ref[slot * held + pair]
    for frame in range(frames):
        own_edge_ref[0, frame] = mine_ref[frame, pair]
        own_edge_ref[1, frame] = other_ref[(CACHE + frame) * held + pair]


def finish(mine_ref, other_ref, live, first, pairs, value, targets):
    _, held, side, _ = mine_ref.shape
    frames, channels = value.shape[0], value.shape[-1]
    start, count = pairs
    near, far = halves(lax.axis_index("wa"), value[:, :, :side], value[:, :, side:])
    for mine, value, target in ((True, near, targets[0]), (False, far, targets[1])):
        for frame in range(frames):
            for k in range(count):
                if mine:
                    raw = mine_ref[first + frame, start + k]
                else:
                    raw = other_ref[(CACHE + first + frame) * held + start + k]
                raw = raw.astype(jnp.float32)
                high = raw[:, 2 * LANES:]
                for row, tail in ((0, high), (1, pltpu.roll(high, LANES // 2, 1))):
                    low = raw[:, row * LANES:(row + 1) * LANES]
                    features = jnp.concatenate([low, tail[:, :channels - LANES]], axis=-1)
                    summed = features + value[frame, 2 * k + row]
                    kept = jnp.where(live[first + frame].reshape(1, 1) > 0.5, summed, 0.0)
                    target(first + frame, 2 * k + row, kept.astype(jnp.bfloat16))


def middle_kernel(
    marks_ref, tail_mine_ref, tail_other_ref, mine_ref, other_ref,
    gain1_ref, w1_ref, bias1_ref, gain2_ref, w2_ref, bias2_ref,
    near_ref, inner_ref, keep_ref, send_ref, operand,
):
    core = lax.axis_index("wa")
    frames, pairs, side, packed = mine_ref.shape
    channels = w1_ref.shape[-1]
    rows = 2 * pairs
    tiles = CACHE * pairs
    live = frame_flags(marks_ref[...], range(frames))
    earlier = lax.axis_index("tchunk") > 0

    def unpacked(ref, start, count):
        return ref[start:start + count * pairs].reshape(count, pairs, side, packed)

    def hide(first, count, flags):
        def then(start, part, hidden):
            flag = jnp.concatenate(flags[start:start + part], axis=0)
            inner_ref[first + start:first + start + part] = second_rows(hidden, flag, gain2_ref, channels)

        convolved(operand, w1_ref, bias1_ref, first, count, rows - 2, then)

    @pl.when(earlier)
    def _():
        fill_rows(
            operand, 0, unpacked(tail_mine_ref, 0, CACHE), unpacked(tail_other_ref, 0, CACHE), gain1_ref, channels
        )
        hide(0, 2, frame_flags(tail_mine_ref[tiles], range(CACHE - 2, CACHE)))

    @pl.when(jnp.logical_not(earlier))
    def _():
        operand[0:CACHE] = jnp.zeros((CACHE,) + operand.shape[1:], operand.dtype)
        inner_ref[0:2] = jnp.zeros((2,) + inner_ref.shape[1:], inner_ref.dtype)

    fill_rows(operand, CACHE, mine_ref[...], unpacked(other_ref, tiles, frames), gain1_ref, channels)
    near_ref[...] = operand[:, pl.ds((rows - 2) * core, 2)]
    hide(2, frames, live)

    def put(ref):
        def store(frame, row, value):
            ref[frame, row] = value
        return store

    def then(start, part, result):
        finish(mine_ref, other_ref, live, start, (1, pairs - 2), result, (put(keep_ref), put(send_ref)))

    convolved(inner_ref, w2_ref, bias2_ref, 0, frames, rows - 4, then)


def outer_kernel(
    marks_ref, tail_mine_ref, mine_ref, other_ref, tail_edge_ref, own_edge_ref, near_ref, inner_ref,
    keep_mid_ref, send_mid_ref, gain1_ref, w1_ref, bias1_ref, gain2_ref, w2_ref, bias2_ref,
    keep_ref, send_ref, strip, operand,
):
    core, place = lax.axis_index("wa"), lax.axis_index("ha")
    frames, pairs = mine_ref.shape[:2]
    inner_rows = inner_ref.shape[1]
    channels = w1_ref.shape[-1]
    outward, inward = pl.ds(2 * core, 2), pl.ds(2 * (1 - core), 2)

    for start, ref in ((0, tail_edge_ref), (CACHE, own_edge_ref)):
        left, right = halves(core, ref[1], ref[0])
        upper, lower = first_rows(left[:, None], right[:, None], gain1_ref, channels)
        strip[start:start + ref.shape[1], pl.ds(2 * core, 1)] = upper
        strip[start:start + ref.shape[1], pl.ds(2 * core + 1, 1)] = lower
    strip[:, inward] = near_ref[...]
    inside = jnp.where(core == 0, place > 0, place < lax.axis_size("ha") - 1)
    row = lax.broadcasted_iota(jnp.int32, (1, 2, 1, 1), 1)
    row_flag = jnp.where((row == core) & jnp.logical_not(inside), 0.0, 1.0)
    live = frame_flags(marks_ref[...], range(frames))
    flags = frame_flags(tail_mine_ref[CACHE * pairs], range(CACHE - 2, CACHE)) + live
    operand[:, inward] = inner_ref[:, pl.ds((inner_rows - 2) * core, 2)]

    def hide(start, part, hidden):
        flag = jnp.concatenate(flags[start:start + part], axis=0) * row_flag
        operand[start:start + part, outward] = second_rows(hidden, flag, gain2_ref, channels)

    convolved(strip, w1_ref, bias1_ref, 0, frames + 2, 2, hide)

    def put(ref):
        def store(frame, row, value):
            ref[frame, (inner_rows - 2) * core + row] = value
        return store

    def then(start, part, result):
        finish(mine_ref, other_ref, live, start, ((pairs - 1) * core, 1), result, (put(keep_ref), put(send_ref)))

    convolved(operand, w2_ref, bias2_ref, 0, frames, 2, then)
    for source, target in ((keep_mid_ref, keep_ref), (send_mid_ref, send_ref)):
        target[:, pl.ds(2 * (1 - core), inner_rows - 2)] = source[...]


def shards(features, frame_counts, gain_first, conv_first, bias_first, gain_second, conv_second, bias_second):
    frames, rows, side, channels = features.shape
    pairs, half = rows // 2, rows // 2
    held = half // 2 + 1
    tall, cores, blocks = lax.axis_size("ha"), lax.axis_size("wa"), lax.axis_size("tchunk")
    packed, width, tiles = 3 * LANES, 2 * side, CACHE * held
    bf16 = jnp.bfloat16
    vmem = pl.BlockSpec(memory_space=pltpu.VMEM)
    limit = pltpu.CompilerParams(vmem_limit_bytes=20 * 2**20)
    work = 2 * TAPS**3 * channels * channels * width

    def shape(*extent):
        return jax.ShapeDtypeStruct(extent, bf16)

    def cost(flops, fetched):
        return pl.CostEstimate(flops=flops, bytes_accessed=fetched, transcendentals=0)

    slots = pl.pallas_call(
        slots_kernel,
        out_shape=jax.ShapeDtypeStruct((side, packed), jnp.int32),
        out_specs=vmem,
        compiler_params=limit,
        cost_estimate=cost(2**34, 2**20),
    )()
    slots, frame_counts = lax.optimization_barrier((slots, frame_counts))
    tail, mine, theirs, marks = pl.pallas_call(
        prepare_kernel,
        out_shape=(
            shape(tiles + 1, side, packed), shape(frames, held, side, packed),
            shape((CACHE + frames) * held, side, packed), shape(side, packed),
        ),
        in_specs=[pl.BlockSpec(memory_space=pltpu.SMEM), vmem, vmem],
        out_specs=(vmem,) * 4,
        scratch_shapes=[pltpu.VMEM((frames, pairs, side, packed), bf16)],
        compiler_params=limit,
    )(frame_counts, slots, features)

    tail, tail_theirs = joined_tails(tail, theirs[:tiles])
    if blocks > 2:
        theirs = jnp.concatenate([tail_theirs, theirs[tiles:]], axis=0)
    straight, crossed, diagonal, across = [], [], [], []

    def index(block, h, core):
        return (block * tall + h) * cores + core

    for h in range(tall):
        for k in range(blocks - 1):
            for core in range(cores):
                straight.append((index(k, h, core), index(k + 1, h, core)))
                crossed.append((index(k, h, core), index(k + 1, h, 1 - core)))
    for h in range(tall - 1):
        for k in range(blocks):
            lower, upper = index(k, h, 1), index(k, h + 1, 0)
            across += [(lower, upper), (upper, lower)]
            if k + 1 < blocks:
                lower_next, upper_next = index(k + 1, h, 1), index(k + 1, h + 1, 0)
                diagonal += [(lower, upper_next), (upper, lower_next)]
    axes = ("tchunk", "ha", "wa")
    swap = [(0, 1), (1, 0)]
    tail_mine = lax.ppermute(tail, axes, straight)
    tail_other = lax.ppermute(tail_theirs, axes, crossed)
    other = lax.ppermute(theirs, "wa", swap)
    tail_edge, own_edge = pl.pallas_call(
        border_kernel,
        out_shape=(shape(2, CACHE, side, packed), shape(2, frames, side, packed)),
        in_specs=[vmem] * 3,
        out_specs=(vmem, vmem),
        compiler_params=limit,
        cost_estimate=cost(2**34, 2**20),
    )(tail, mine, other)
    own_edge = lax.ppermute(own_edge, axes, across)
    tail_edge = lax.ppermute(tail_edge, axes, diagonal)

    weights = (
        gain_first.reshape(1, channels), conv_first, bias_first.reshape(1, channels),
        gain_second.reshape(1, channels), conv_second, bias_second.reshape(1, channels),
    )
    near, inner, keep, send = pl.pallas_call(
        middle_kernel,
        out_shape=(
            shape(frames + CACHE, 2, width, packed), shape(frames + 2, half, width, packed),
            shape(frames, half - 2, side, channels), shape(frames, half - 2, side, channels),
        ),
        in_specs=[vmem] * 11,
        out_specs=(vmem,) * 4,
        scratch_shapes=[pltpu.VMEM((frames + CACHE, half + 2, width, packed), bf16)],
        compiler_params=limit,
        cost_estimate=cost(work * ((frames + 2) * half + frames * (half - 2)), 8 * 2**20),
    )(marks, tail_mine, tail_other, mine, other, *weights)
    keep, send = pl.pallas_call(
        outer_kernel,
        out_shape=(shape(frames, half, side, channels), shape(frames, half, side, channels)),
        in_specs=[vmem] * 16,
        out_specs=(vmem, vmem),
        scratch_shapes=[
            pltpu.VMEM((frames + CACHE, 4, width, packed), bf16),
            pltpu.VMEM((frames + 2, 4, width, packed), bf16),
        ],
        compiler_params=limit,
        cost_estimate=cost(work * 2 * (2 * frames + 2), 8 * 2**20),
    )(marks, tail_mine, mine, other, tail_edge, own_edge, near, inner, keep, send, *weights)
    got = lax.ppermute(send, "wa", swap)
    upper, lower = halves(lax.axis_index("wa"), keep, got)
    return jnp.concatenate([upper, lower], axis=1)


def solution(mesh):
    return jax.shard_map(
        shards,
        mesh=mesh,
        in_specs=(
            P(("grp", "tchunk"), "ha", "wa", None),
            P(("grp", "tchunk")),
            P(), P(), P(), P(), P(), P(),
        ),
        out_specs=P(("grp", "tchunk"), "ha", "wa", None),
        check_vma=False,
    )
```

profile of v0, /device:TPU:0, one launch (start us, length us, event | category | flops | bytes accessed | tf_op | source)
XLA Modules:
  0.0 24.4 jit_solution(15624862287684197814)
XLA Ops:
  0.0 0.0 copy-start.2
  0.7 0.3 %copy-done.2 = bf16[8,8,8,192]{3,2,1,0:T(8,128)(2,1)S(1)} copy-done((bf16[8,8,8,192]{3,2,1,0:T(8,128)(2,1)S(1)}, bf16[8,8,8,192]{3,2,1,0:T(8,128)(2,1)}, u32[]{:S(2)}) %copy-start.2) | copy-done | bytes 196632
  1.0 0.1 shard_map.83
  1.1 0.5 %collective-permute-start.1 = (bf16[36,8,384]{2,1,0:T(8,128)(2,1)S(1)}, bf16[36,8,384]{2,1,0:T(8,128)(2,1)S(1)}, u32[]{:S(2)}, u32[]{:S(2)}) collective-permute-start(bf16[36,8,384]{2,1,0:T(8,128)(2,1)S(1)} %get-tuple-element.24), channel_id=1, source_target_pairs={{0,1},{1,0},{2,3},{3,2},{4,5},{5,4},{6,7},{7,6},{8,9},{9,8},{10,11... | collective-permute-start | bytes 663560 | tf_op jit(solution)/shard_map/ppermute | solution.py:374
  1.6 4.4 %collective-permute-start = (bf16[13,8,384]{2,1,0:T(8,128)(2,1)S(1)}, bf16[13,8,384]{2,1,0:T(8,128)(2,1)S(1)}, u32[]{:S(2)}, u32[]{:S(2)}) collective-permute-start(bf16[13,8,384]{2,1,0:T(8,128)(2,1)S(1)} %get-tuple-element.22.tail_ref), channel_id=1, source_target_pairs={{0,8},{1,9},{2,10},{3,11},{4,12},{5,13},{6,14},{7,15},{16,24},{17,... | collective-permute-start | bytes 239624 | tf_op jit(solution)/shard_map/ppermute | solution.py:372
  6.1 1.4 %collective-permute-start.4 = (bf16[12,8,384]{2,1,0:T(8,128)(2,1)S(1)}, bf16[12,8,384]{2,1,0:T(8,128)(2,1)S(1)}, u32[]{:S(2)}, u32[]{:S(2)}) collective-permute-start(bf16[12,8,384]{2,1,0:T(8,128)(2,1)S(1)} %slice.3), channel_id=1, source_target_pairs={{0,9},{1,8},{2,11},{3,10},{4,13},{5,12},{6,15},{7,14},{16,25},{17,... | collective-permute-start | bytes 221192 | tf_op jit(solution)/shard_map/ppermute | solution.py:373
  7.5 0.0 collective-permute-done.1.other_ref
  7.5 0.0 copy-start
  7.5 0.0 copy-start.1
  7.5 0.0 copy-start.3
  7.5 0.0 copy-start.4
  7.5 0.0 copy-start.5
  7.5 0.0 copy-start.6
  7.6 0.8 %collective-permute-start.3 = (bf16[2,8,8,384]{3,2,1,0:T(8,128)(2,1)S(1)}, bf16[2,8,8,384]{3,2,1,0:T(8,128)(2,1)S(1)}, u32[]{:S(2)}, u32[]{:S(2)}) collective-permute-start(bf16[2,8,8,384]{3,2,1,0:T(8,128)(2,1)S(1)} %get-tuple-element.26), channel_id=1, source_target_pairs={{1,2},{2,1},{9,10},{10,9},{3,4},{4,3},{11,12},{12,11},{5,6},{6,5},... | collective-permute-start | bytes 294920 | tf_op jit(solution)/shard_map/ppermute | solution.py:383
  8.4 0.8 %collective-permute-start.2 = (bf16[2,4,8,384]{3,2,1,0:T(8,128)(2,1)S(1)}, bf16[2,4,8,384]{3,2,1,0:T(8,128)(2,1)S(1)}, u32[]{:S(2)}, u32[]{:S(2)}) collective-permute-start(bf16[2,4,8,384]{3,2,1,0:T(8,128)(2,1)S(1)} %get-tuple-element.25), channel_id=1, source_target_pairs={{1,10},{2,9},{3,12},{4,11},{5,14},{6,13},{17,26},{18,25},{19,28},{... | collective-permute-start | bytes 147464 | tf_op jit(solution)/shard_map/ppermute | solution.py:384
  9.2 0.7 %collective-permute-done.4.tail_other_ref = bf16[12,8,384]{2,1,0:T(8,128)(2,1)S(1)} collective-permute-done((bf16[12,8,384]{2,1,0:T(8,128)(2,1)S(1)}, bf16[12,8,384]{2,1,0:T(8,128)(2,1)S(1)}, u32[]{:S(2)}, u32[]{:S(2)}) %collective-permute-start.4) | collective-permute-done | bytes 73760 | tf_op jit(solution)/shard_map/ppermute | solution.py:373
  9.9 0.0 collective-permute-done.tail_mine_ref
  9.9 0.0 copy-done
  9.9 0.1 copy-done.1
  10.0 0.0 copy-done.3
  10.0 0.0 copy-done.4
  10.0 0.0 copy-done.5
  10.0 0.0 copy-done.6
  10.0 5.8 %shard_map.85 = (bf16[12,2,16,384]{3,2,1,0:T(8,128)(2,1)S(1)}, bf16[10,4,16,384]{3,2,1,0:T(8,128)(2,1)S(1)}, bf16[8,2,8,192]{3,2,1,0:T(8,128)(2,1)S(1)}, bf16[8,2,8,192]{3,2,1,0:T(8,128)(2,1)S(1)}) custom-call(bf16[8,384]{1,0:T(8,128)(2,1)S(1)} %get-tuple-element.21.marks_ref, bf16[13,8,384]{2,1,0:T(8,128)(2,1)S(1)} %collective-permute-done.tail_mine_ref, ...), custom_call_target="tpu_custom_call" | custom-call | flops 1783627776 | bytes 8388608 | tf_op jit(solution)/shard_map/pallas_call | solution.py:390
  15.9 0.0 collective-permute-done.2.tail_edge_ref
  15.9 0.0 collective-permute-done.3.own_edge_ref
  15.9 3.9 %shard_map.86 = (bf16[8,4,8,192]{3,2,1,0:T(8,128)(2,1)S(1)}, bf16[8,4,8,192]{3,2,1,0:T(8,128)(2,1)S(1)}) custom-call(bf16[8,384]{1,0:T(8,128)(2,1)S(1)} %get-tuple-element.21.marks_ref, bf16[13,8,384]{2,1,0:T(8,128)(2,1)S(1)} %collective-permute-done.tail_mine_ref, bf16[8,3,8,384]{3,2,1,0:T(8,128)(2,1)S(1)} %get-tuple-element.23.mine_ref, ...), custom_call_target="tpu_custom_call" | custom-call | flops 1146617856 | bytes 8388608 | tf_op jit(solution)/shard_map/pallas_call | solution.py:402
  19.8 2.9 %collective-permute-start.5 = (bf16[8,4,8,192]{3,2,1,0:T(8,128)(2,1)S(1)}, bf16[8,4,8,192]{3,2,1,0:T(8,128)(2,1)S(1)}, u32[]{:S(2)}, u32[]{:S(2)}) collective-permute-start(bf16[8,4,8,192]{3,2,1,0:T(8,128)(2,1)S(1)} %get-tuple-element.32), channel_id=1, source_target_pairs={{0,1},{1,0},{2,3},{3,2},{4,5},{5,4},{6,7},{7,6},{8,9},{9,8},{10,11... | collective-permute-start | bytes 294920 | tf_op jit(solution)/shard_map/ppermute | solution.py:414
  22.7 1.0 %collective-permute-done.5 = bf16[8,4,8,192]{3,2,1,0:T(8,128)(2,1)S(1)} collective-permute-done((bf16[8,4,8,192]{3,2,1,0:T(8,128)(2,1)S(1)}, bf16[8,4,8,192]{3,2,1,0:T(8,128)(2,1)S(1)}, u32[]{:S(2)}, u32[]{:S(2)}) %collective-permute-start.5) | collective-permute-done | bytes 98336 | tf_op jit(solution)/shard_map/ppermute | solution.py:414
  23.7 0.7 %pad_maximum_fusion = bf16[8,8,8,192]{3,2,1,0:T(8,128)(2,1)} fusion(bf16[8,4,8,192]{3,2,1,0:T(8,128)(2,1)S(1)} %get-tuple-element.34, bf16[8,4,8,192]{3,2,1,0:T(8,128)(2,1)S(1)} %get-tuple-element.33), kind=kLoop, calls=%fused_computation | loop fusion | flops 98304 | bytes 393216 | tf_op jit(solution)/shard_map/concatenate | solution.py:416
  (4 shorter events, 0.1 us)
Async XLA Ops:
  0.0 1.0 %copy-start.2 = (bf16[8,8,8,192]{3,2,1,0:T(8,128)(2,1)S(1)}, bf16[8,8,8,192]{3,2,1,0:T(8,128)(2,1)}, u32[]{:S(2)}) copy-start(bf16[8,8,8,192]{3,2,1,0:T(8,128)(2,1)} %raw.1) | copy-start | bytes 589828
  1.1 6.3 %collective-permute-start.1 = (bf16[36,8,384]{2,1,0:T(8,128)(2,1)S(1)}, bf16[36,8,384]{2,1,0:T(8,128)(2,1)S(1)}, u32[]{:S(2)}, u32[]{:S(2)}) collective-permute-start(bf16[36,8,384]{2,1,0:T(8,128)(2,1)S(1)} %get-tuple-element.24), channel_id=1, source_target_pairs={{0,1},{1,0},{2,3},{3,2},{4,5},{5,4},{6,7},{7,6},{8,9},{9,8},{10,11... | collective-permute-start | bytes 663560 | tf_op jit(solution)/shard_map/ppermute | solution.py:374
  1.6 8.3 %collective-permute-start = (bf16[13,8,384]{2,1,0:T(8,128)(2,1)S(1)}, bf16[13,8,384]{2,1,0:T(8,128)(2,1)S(1)}, u32[]{:S(2)}, u32[]{:S(2)}) collective-permute-start(bf16[13,8,384]{2,1,0:T(8,128)(2,1)S(1)} %get-tuple-element.22.tail_ref), channel_id=1, source_target_pairs={{0,8},{1,9},{2,10},{3,11},{4,12},{5,13},{6,14},{7,15},{16,24},{17,... | collective-permute-start | bytes 239624 | tf_op jit(solution)/shard_map/ppermute | solution.py:372
  6.1 3.8 %collective-permute-start.4 = (bf16[12,8,384]{2,1,0:T(8,128)(2,1)S(1)}, bf16[12,8,384]{2,1,0:T(8,128)(2,1)S(1)}, u32[]{:S(2)}, u32[]{:S(2)}) collective-permute-start(bf16[12,8,384]{2,1,0:T(8,128)(2,1)S(1)} %slice.3), channel_id=1, source_target_pairs={{0,9},{1,8},{2,11},{3,10},{4,13},{5,12},{6,15},{7,14},{16,25},{17,... | collective-permute-start | bytes 221192 | tf_op jit(solution)/shard_map/ppermute | solution.py:373
  7.5 2.5 %copy-start = (bf16[3,3,3,192,192]{4,3,2,1,0:T(8,128)(2,1)S(1)}, bf16[3,3,3,192,192]{4,3,2,1,0:T(8,128)(2,1)}, u32[]{:S(2)}) copy-start(bf16[3,3,3,192,192]{4,3,2,1,0:T(8,128)(2,1)} %w1_ref.3) | copy-start | bytes 5971972
  7.5 2.5 %copy-start.1 = (bf16[3,3,3,192,192]{4,3,2,1,0:T(8,128)(2,1)S(1)}, bf16[3,3,3,192,192]{4,3,2,1,0:T(8,128)(2,1)}, u32[]{:S(2)}) copy-start(bf16[3,3,3,192,192]{4,3,2,1,0:T(8,128)(2,1)} %w2_ref.3) | copy-start | bytes 5971972
  7.5 2.5 %copy-start.3 = (f32[192]{0:T(256)S(1)}, f32[192]{0:T(256)}, u32[]{:S(2)}) copy-start(f32[192]{0:T(256)} %param.10) | copy-start | bytes 2308
  7.5 2.5 %copy-start.4 = (f32[192]{0:T(256)S(1)}, f32[192]{0:T(256)}, u32[]{:S(2)}) copy-start(f32[192]{0:T(256)} %param.12) | copy-start | bytes 2308
  7.5 2.5 %copy-start.5 = (f32[192]{0:T(256)S(1)}, f32[192]{0:T(256)}, u32[]{:S(2)}) copy-start(f32[192]{0:T(256)} %param.13) | copy-start | bytes 2308
  7.5 2.5 %copy-start.6 = (f32[192]{0:T(256)S(1)}, f32[192]{0:T(256)}, u32[]{:S(2)}) copy-start(f32[192]{0:T(256)} %param.15) | copy-start | bytes 2308
  7.6 8.3 %collective-permute-start.3 = (bf16[2,8,8,384]{3,2,1,0:T(8,128)(2,1)S(1)}, bf16[2,8,8,384]{3,2,1,0:T(8,128)(2,1)S(1)}, u32[]{:S(2)}, u32[]{:S(2)}) collective-permute-start(bf16[2,8,8,384]{3,2,1,0:T(8,128)(2,1)S(1)} %get-tuple-element.26), channel_id=1, source_target_pairs={{1,2},{2,1},{9,10},{10,9},{3,4},{4,3},{11,12},{12,11},{5,6},{6,5},... | collective-permute-start | bytes 294920 | tf_op jit(solution)/shard_map/ppermute | solution.py:383
  8.4 7.5 %collective-permute-start.2 = (bf16[2,4,8,384]{3,2,1,0:T(8,128)(2,1)S(1)}, bf16[2,4,8,384]{3,2,1,0:T(8,128)(2,1)S(1)}, u32[]{:S(2)}, u32[]{:S(2)}) collective-permute-start(bf16[2,4,8,384]{3,2,1,0:T(8,128)(2,1)S(1)} %get-tuple-element.25), channel_id=1, source_target_pairs={{1,10},{2,9},{3,12},{4,11},{5,14},{6,13},{17,26},{18,25},{19,28},{... | collective-permute-start | bytes 147464 | tf_op jit(solution)/shard_map/ppermute | solution.py:384
  19.8 3.8 %collective-permute-start.5 = (bf16[8,4,8,192]{3,2,1,0:T(8,128)(2,1)S(1)}, bf16[8,4,8,192]{3,2,1,0:T(8,128)(2,1)S(1)}, u32[]{:S(2)}, u32[]{:S(2)}) collective-permute-start(bf16[8,4,8,192]{3,2,1,0:T(8,128)(2,1)S(1)} %get-tuple-element.32), channel_id=1, source_target_pairs={{0,1},{1,0},{2,3},{3,2},{4,5},{5,4},{6,7},{7,6},{8,9},{9,8},{10,11... | collective-permute-start | bytes 294920 | tf_op jit(solution)/shard_map/ppermute | solution.py:414
where the time goes:
time: 24.6 us; the launch traced here: 24.4 us
  starting transfers between devices  10.8 us (44%)
  Pallas kernels  9.91 us (40%)
  waiting for transfers between devices  1.73 us (7%)
  between operations  0.84 us (3%)
  other arithmetic  0.77 us (3%)
  local copies, waits for them, and re-layouts  0.41 us (2%)
    pallas_call x1, Pallas kernels, shards(): pl.pallas_call(middle_kernel, out_shape=(shape(frames + CACHE, 2, width,...  5.81 us
    ppermute x1, starting transfers between devices, shards(): tail_mine = lax.ppermute(tail, axes, straight)  4.41 us
    pallas_call x1, Pallas kernels, shards(): pl.pallas_call(outer_kernel, out_shape=(shape(frames, half, side, channel...  3.92 us
    ppermute x1, starting transfers between devices, shards(): got = lax.ppermute(send, 'wa', swap)  2.86 us
    ppermute x1, starting transfers between devices, shards(): tail_other = lax.ppermute(tail_theirs, axes, crossed)  1.38 us
    ppermute x1, waiting for transfers between devices, shards(): got = lax.ppermute(send, 'wa', swap)  0.99 us
    ppermute x1, starting transfers between devices, shards(): own_edge = lax.ppermute(own_edge, axes, across)  0.8 us
    ppermute x1, starting transfers between devices, shards(): tail_edge = lax.ppermute(tail_edge, axes, diagonal)  0.8 us
  transfers between devices with their start and end apart: 6, of which 2 were waited for; matrix products, arithmetic and copies ran while one was open for 0% of the time, Pallas kernels for 24%

commit v1 on v0

--- a/solution.py
+++ b/solution.py
@@ -9,7 +9,7 @@
 CACHE = 4
 TAPS = 3
 LANES = 128
-PRODUCT = 64
+PRODUCT = 192
 
 
 def slots_kernel(slots_ref):
@@ -127,7 +127,8 @@
 
 
 def convolved(operand, weights_ref, bias_ref, frame, frames, rows, then):
-    step = max(1, PRODUCT // (rows * operand.shape[2]))
+    products = -(-frames * rows * operand.shape[2] // PRODUCT)
+    step = -(-frames // products)
     for start in range(0, frames, step):
         count = min(step, frames - start)
         then(start, count, convolved_part(operand, weights_ref, bias_ref, frame + start, count, rows))

time: 24.6 us -> 20.4 us (0.83)
  Pallas kernels: 9.91 us -> 5.72 us
    pallas_call x1, Pallas kernels: 5.81 us -> 2.97 us  [shards(): pl.pallas_call(middle_kernel, out_shape=(shape(frames + CACHE, 2, width,...]
    pallas_call x1, Pallas kernels: 3.92 us -> 2.56 us  [shards(): pl.pallas_call(outer_kernel, out_shape=(shape(frames, half, side, channel...]
  transfers between devices with their start and end apart: 6 -> 6, of which waited for: 2 -> 2; matrix products, arithmetic and copies ran while one was open for 0% -> 0% of each run, Pallas kernels for 24% -> 15%
where the time goes in v1:
time: 20.4 us; the launch traced here: 20.2 us
  starting transfers between devices  10.8 us (53%)
  Pallas kernels  5.72 us (28%)
  waiting for transfers between devices  1.73 us (8%)
  between operations  0.84 us (4%)
  other arithmetic  0.77 us (4%)
  local copies, waits for them, and re-layouts  0.41 us (2%)
    ppermute x1, starting transfers between devices, shards(): tail_mine = lax.ppermute(tail, axes, straight)  4.41 us
    pallas_call x1, Pallas kernels, shards(): pl.pallas_call(middle_kernel, out_shape=(shape(frames + CACHE, 2, width,...  2.97 us
    ppermute x1, starting transfers between devices, shards(): got = lax.ppermute(send, 'wa', swap)  2.87 us
    pallas_call x1, Pallas kernels, shards(): pl.pallas_call(outer_kernel, out_shape=(shape(frames, half, side, channel...  2.56 us
    ppermute x1, starting transfers between devices, shards(): tail_other = lax.ppermute(tail_theirs, axes, crossed)  1.38 us
    ppermute x1, waiting for transfers between devices, shards(): got = lax.ppermute(send, 'wa', swap)  0.99 us
    ppermute x1, starting transfers between devices, shards(): own_edge = lax.ppermute(own_edge, axes, across)  0.8 us
    ppermute x1, starting transfers between devices, shards(): tail_edge = lax.ppermute(tail_edge, axes, diagonal)  0.8 us
  transfers between devices with their start and end apart: 6, of which 2 were waited for; matrix products, arithmetic and copies ran while one was open for 0% of the time, Pallas kernels for 15%

profile of v1, /device:TPU:0, one launch (start us, length us, event | category | flops | bytes accessed | tf_op | source)
XLA Modules:
  0.0 20.2 jit_solution(7359801616404854107)
XLA Ops:
  0.0 0.0 copy-start.2
  0.7 0.3 %copy-done.2 = bf16[8,8,8,192]{3,2,1,0:T(8,128)(2,1)S(1)} copy-done((bf16[8,8,8,192]{3,2,1,0:T(8,128)(2,1)S(1)}, bf16[8,8,8,192]{3,2,1,0:T(8,128)(2,1)}, u32[]{:S(2)}) %copy-start.2) | copy-done | bytes 196632
  1.0 0.1 shard_map.83
  1.1 0.5 %collective-permute-start.1 = (bf16[36,8,384]{2,1,0:T(8,128)(2,1)S(1)}, bf16[36,8,384]{2,1,0:T(8,128)(2,1)S(1)}, u32[]{:S(2)}, u32[]{:S(2)}) collective-permute-start(bf16[36,8,384]{2,1,0:T(8,128)(2,1)S(1)} %get-tuple-element.24), channel_id=1, source_target_pairs={{0,1},{1,0},{2,3},{3,2},{4,5},{5,4},{6,7},{7,6},{8,9},{9,8},{10,11... | collective-permute-start | bytes 663560 | tf_op jit(solution)/shard_map/ppermute | solution.py:375
  1.6 4.4 %collective-permute-start = (bf16[13,8,384]{2,1,0:T(8,128)(2,1)S(1)}, bf16[13,8,384]{2,1,0:T(8,128)(2,1)S(1)}, u32[]{:S(2)}, u32[]{:S(2)}) collective-permute-start(bf16[13,8,384]{2,1,0:T(8,128)(2,1)S(1)} %get-tuple-element.22.tail_ref), channel_id=1, source_target_pairs={{0,8},{1,9},{2,10},{3,11},{4,12},{5,13},{6,14},{7,15},{16,24},{17,... | collective-permute-start | bytes 239624 | tf_op jit(solution)/shard_map/ppermute | solution.py:373
  6.1 1.4 %collective-permute-start.4 = (bf16[12,8,384]{2,1,0:T(8,128)(2,1)S(1)}, bf16[12,8,384]{2,1,0:T(8,128)(2,1)S(1)}, u32[]{:S(2)}, u32[]{:S(2)}) collective-permute-start(bf16[12,8,384]{2,1,0:T(8,128)(2,1)S(1)} %slice.3), channel_id=1, source_target_pairs={{0,9},{1,8},{2,11},{3,10},{4,13},{5,12},{6,15},{7,14},{16,25},{17,... | collective-permute-start | bytes 221192 | tf_op jit(solution)/shard_map/ppermute | solution.py:374
  7.5 0.0 collective-permute-done.1.other_ref
  7.5 0.0 copy-start
  7.5 0.0 copy-start.1
  7.5 0.0 copy-start.3
  7.5 0.0 copy-start.4
  7.5 0.0 copy-start.5
  7.5 0.0 copy-start.6
  7.6 0.8 %collective-permute-start.3 = (bf16[2,8,8,384]{3,2,1,0:T(8,128)(2,1)S(1)}, bf16[2,8,8,384]{3,2,1,0:T(8,128)(2,1)S(1)}, u32[]{:S(2)}, u32[]{:S(2)}) collective-permute-start(bf16[2,8,8,384]{3,2,1,0:T(8,128)(2,1)S(1)} %get-tuple-element.26), channel_id=1, source_target_pairs={{1,2},{2,1},{9,10},{10,9},{3,4},{4,3},{11,12},{12,11},{5,6},{6,5},... | collective-permute-start | bytes 294920 | tf_op jit(solution)/shard_map/ppermute | solution.py:384
  8.4 0.8 %collective-permute-start.2 = (bf16[2,4,8,384]{3,2,1,0:T(8,128)(2,1)S(1)}, bf16[2,4,8,384]{3,2,1,0:T(8,128)(2,1)S(1)}, u32[]{:S(2)}, u32[]{:S(2)}) collective-permute-start(bf16[2,4,8,384]{3,2,1,0:T(8,128)(2,1)S(1)} %get-tuple-element.25), channel_id=1, source_target_pairs={{1,10},{2,9},{3,12},{4,11},{5,14},{6,13},{17,26},{18,25},{19,28},{... | collective-permute-start | bytes 147464 | tf_op jit(solution)/shard_map/ppermute | solution.py:385
  9.2 0.7 %collective-permute-done.4.tail_other_ref = bf16[12,8,384]{2,1,0:T(8,128)(2,1)S(1)} collective-permute-done((bf16[12,8,384]{2,1,0:T(8,128)(2,1)S(1)}, bf16[12,8,384]{2,1,0:T(8,128)(2,1)S(1)}, u32[]{:S(2)}, u32[]{:S(2)}) %collective-permute-start.4) | collective-permute-done | bytes 73760 | tf_op jit(solution)/shard_map/ppermute | solution.py:374
  9.9 0.0 collective-permute-done.tail_mine_ref
  9.9 0.0 copy-done
  9.9 0.1 copy-done.1
  10.0 0.0 copy-done.3
  10.0 0.0 copy-done.4
  10.0 0.0 copy-done.5
  10.0 0.0 copy-done.6
  10.0 3.0 %shard_map.85 = (bf16[12,2,16,384]{3,2,1,0:T(8,128)(2,1)S(1)}, bf16[10,4,16,384]{3,2,1,0:T(8,128)(2,1)S(1)}, bf16[8,2,8,192]{3,2,1,0:T(8,128)(2,1)S(1)}, bf16[8,2,8,192]{3,2,1,0:T(8,128)(2,1)S(1)}) custom-call(bf16[8,384]{1,0:T(8,128)(2,1)S(1)} %get-tuple-element.21.marks_ref, bf16[13,8,384]{2,1,0:T(8,128)(2,1)S(1)} %collective-permute-done.tail_mine_ref, ...), custom_call_target="tpu_custom_call" | custom-call | flops 1783627776 | bytes 8388608 | tf_op jit(solution)/shard_map/pallas_call | solution.py:391
  13.0 0.0 collective-permute-done.2.tail_edge_ref
  13.0 0.0 collective-permute-done.3.own_edge_ref
  13.0 2.6 %shard_map.86 = (bf16[8,4,8,192]{3,2,1,0:T(8,128)(2,1)S(1)}, bf16[8,4,8,192]{3,2,1,0:T(8,128)(2,1)S(1)}) custom-call(bf16[8,384]{1,0:T(8,128)(2,1)S(1)} %get-tuple-element.21.marks_ref, bf16[13,8,384]{2,1,0:T(8,128)(2,1)S(1)} %collective-permute-done.tail_mine_ref, bf16[8,3,8,384]{3,2,1,0:T(8,128)(2,1)S(1)} %get-tuple-element.23.mine_ref, ...), custom_call_target="tpu_custom_call" | custom-call | flops 1146617856 | bytes 8388608 | tf_op jit(solution)/shard_map/pallas_call | solution.py:403
  15.6 2.9 %collective-permute-start.5 = (bf16[8,4,8,192]{3,2,1,0:T(8,128)(2,1)S(1)}, bf16[8,4,8,192]{3,2,1,0:T(8,128)(2,1)S(1)}, u32[]{:S(2)}, u32[]{:S(2)}) collective-permute-start(bf16[8,4,8,192]{3,2,1,0:T(8,128)(2,1)S(1)} %get-tuple-element.32), channel_id=1, source_target_pairs={{0,1},{1,0},{2,3},{3,2},{4,5},{5,4},{6,7},{7,6},{8,9},{9,8},{10,11... | collective-permute-start | bytes 294920 | tf_op jit(solution)/shard_map/ppermute | solution.py:415
  18.5 1.0 %collective-permute-done.5 = bf16[8,4,8,192]{3,2,1,0:T(8,128)(2,1)S(1)} collective-permute-done((bf16[8,4,8,192]{3,2,1,0:T(8,128)(2,1)S(1)}, bf16[8,4,8,192]{3,2,1,0:T(8,128)(2,1)S(1)}, u32[]{:S(2)}, u32[]{:S(2)}) %collective-permute-start.5) | collective-permute-done | bytes 98336 | tf_op jit(solution)/shard_map/ppermute | solution.py:415
  19.5 0.7 %pad_maximum_fusion = bf16[8,8,8,192]{3,2,1,0:T(8,128)(2,1)} fusion(bf16[8,4,8,192]{3,2,1,0:T(8,128)(2,1)S(1)} %get-tuple-element.34, bf16[8,4,8,192]{3,2,1,0:T(8,128)(2,1)S(1)} %get-tuple-element.33), kind=kLoop, calls=%fused_computation | loop fusion | flops 98304 | bytes 393216 | tf_op jit(solution)/shard_map/concatenate | solution.py:417
  (4 shorter events, 0.1 us)
Async XLA Ops:
  0.0 1.0 %copy-start.2 = (bf16[8,8,8,192]{3,2,1,0:T(8,128)(2,1)S(1)}, bf16[8,8,8,192]{3,2,1,0:T(8,128)(2,1)}, u32[]{:S(2)}) copy-start(bf16[8,8,8,192]{3,2,1,0:T(8,128)(2,1)} %raw.1) | copy-start | bytes 589828
  1.1 6.3 %collective-permute-start.1 = (bf16[36,8,384]{2,1,0:T(8,128)(2,1)S(1)}, bf16[36,8,384]{2,1,0:T(8,128)(2,1)S(1)}, u32[]{:S(2)}, u32[]{:S(2)}) collective-permute-start(bf16[36,8,384]{2,1,0:T(8,128)(2,1)S(1)} %get-tuple-element.24), channel_id=1, source_target_pairs={{0,1},{1,0},{2,3},{3,2},{4,5},{5,4},{6,7},{7,6},{8,9},{9,8},{10,11... | collective-permute-start | bytes 663560 | tf_op jit(solution)/shard_map/ppermute | solution.py:375
  1.6 8.3 %collective-permute-start = (bf16[13,8,384]{2,1,0:T(8,128)(2,1)S(1)}, bf16[13,8,384]{2,1,0:T(8,128)(2,1)S(1)}, u32[]{:S(2)}, u32[]{:S(2)}) collective-permute-start(bf16[13,8,384]{2,1,0:T(8,128)(2,1)S(1)} %get-tuple-element.22.tail_ref), channel_id=1, source_target_pairs={{0,8},{1,9},{2,10},{3,11},{4,12},{5,13},{6,14},{7,15},{16,24},{17,... | collective-permute-start | bytes 239624 | tf_op jit(solution)/shard_map/ppermute | solution.py:373
  6.1 3.8 %collective-permute-start.4 = (bf16[12,8,384]{2,1,0:T(8,128)(2,1)S(1)}, bf16[12,8,384]{2,1,0:T(8,128)(2,1)S(1)}, u32[]{:S(2)}, u32[]{:S(2)}) collective-permute-start(bf16[12,8,384]{2,1,0:T(8,128)(2,1)S(1)} %slice.3), channel_id=1, source_target_pairs={{0,9},{1,8},{2,11},{3,10},{4,13},{5,12},{6,15},{7,14},{16,25},{17,... | collective-permute-start | bytes 221192 | tf_op jit(solution)/shard_map/ppermute | solution.py:374
  7.5 2.5 %copy-start = (bf16[3,3,3,192,192]{4,3,2,1,0:T(8,128)(2,1)S(1)}, bf16[3,3,3,192,192]{4,3,2,1,0:T(8,128)(2,1)}, u32[]{:S(2)}) copy-start(bf16[3,3,3,192,192]{4,3,2,1,0:T(8,128)(2,1)} %w1_ref.3) | copy-start | bytes 5971972
  7.5 2.5 %copy-start.1 = (bf16[3,3,3,192,192]{4,3,2,1,0:T(8,128)(2,1)S(1)}, bf16[3,3,3,192,192]{4,3,2,1,0:T(8,128)(2,1)}, u32[]{:S(2)}) copy-start(bf16[3,3,3,192,192]{4,3,2,1,0:T(8,128)(2,1)} %w2_ref.3) | copy-start | bytes 5971972
  7.5 2.5 %copy-start.3 = (f32[192]{0:T(256)S(1)}, f32[192]{0:T(256)}, u32[]{:S(2)}) copy-start(f32[192]{0:T(256)} %param.10) | copy-start | bytes 2308
  7.5 2.5 %copy-start.4 = (f32[192]{0:T(256)S(1)}, f32[192]{0:T(256)}, u32[]{:S(2)}) copy-start(f32[192]{0:T(256)} %param.12) | copy-start | bytes 2308
  7.5 2.5 %copy-start.5 = (f32[192]{0:T(256)S(1)}, f32[192]{0:T(256)}, u32[]{:S(2)}) copy-start(f32[192]{0:T(256)} %param.13) | copy-start | bytes 2308
  7.5 2.5 %copy-start.6 = (f32[192]{0:T(256)S(1)}, f32[192]{0:T(256)}, u32[]{:S(2)}) copy-start(f32[192]{0:T(256)} %param.15) | copy-start | bytes 2308
  7.6 5.5 %collective-permute-start.3 = (bf16[2,8,8,384]{3,2,1,0:T(8,128)(2,1)S(1)}, bf16[2,8,8,384]{3,2,1,0:T(8,128)(2,1)S(1)}, u32[]{:S(2)}, u32[]{:S(2)}) collective-permute-start(bf16[2,8,8,384]{3,2,1,0:T(8,128)(2,1)S(1)} %get-tuple-element.26), channel_id=1, source_target_pairs={{1,2},{2,1},{9,10},{10,9},{3,4},{4,3},{11,12},{12,11},{5,6},{6,5},... | collective-permute-start | bytes 294920 | tf_op jit(solution)/shard_map/ppermute | solution.py:384
  8.4 4.6 %collective-permute-start.2 = (bf16[2,4,8,384]{3,2,1,0:T(8,128)(2,1)S(1)}, bf16[2,4,8,384]{3,2,1,0:T(8,128)(2,1)S(1)}, u32[]{:S(2)}, u32[]{:S(2)}) collective-permute-start(bf16[2,4,8,384]{3,2,1,0:T(8,128)(2,1)S(1)} %get-tuple-element.25), channel_id=1, source_target_pairs={{1,10},{2,9},{3,12},{4,11},{5,14},{6,13},{17,26},{18,25},{19,28},{... | collective-permute-start | bytes 147464 | tf_op jit(solution)/shard_map/ppermute | solution.py:385
  15.6 3.9 %collective-permute-start.5 = (bf16[8,4,8,192]{3,2,1,0:T(8,128)(2,1)S(1)}, bf16[8,4,8,192]{3,2,1,0:T(8,128)(2,1)S(1)}, u32[]{:S(2)}, u32[]{:S(2)}) collective-permute-start(bf16[8,4,8,192]{3,2,1,0:T(8,128)(2,1)S(1)} %get-tuple-element.32), channel_id=1, source_target_pairs={{0,1},{1,0},{2,3},{3,2},{4,5},{5,4},{6,7},{7,6},{8,9},{9,8},{10,11... | collective-permute-start | bytes 294920 | tf_op jit(solution)/shard_map/ppermute | solution.py:415

commit v2 on v1

--- a/solution.py
+++ b/solution.py
@@ -9,7 +9,7 @@
 CACHE = 4
 TAPS = 3
 LANES = 128
-PRODUCT = 192
+PRODUCT = 160
 
 
 def slots_kernel(slots_ref):
@@ -94,6 +94,14 @@
     return pltpu.roll(values.reshape(-1, LANES), LANES // 2, 1).reshape(shape)
 
 
+def shifted(values):
+    width = values.shape[2]
+    column = lax.broadcasted_iota(jnp.int32, (1, 1, width, 1), 2)
+    before = jnp.where(column == 0, 0.0, pltpu.roll(values, 1, 2))
+    after = jnp.where(column == width - 1, 0.0, pltpu.roll(values, width - 1, 2))
+    return before, values, after
+
+
 def first_rows(left, right, gain_ref, channels):
     raw = jnp.concatenate([left.astype(jnp.float32), right.astype(jnp.float32)], axis=2)
     front, back, high = raw[..., :LANES], raw[..., LANES:2 * LANES], raw[..., 2 * LANES:]
@@ -109,9 +117,11 @@
     front = silu(front * scale_front * gain_low)
     back = silu(back * scale_back * gain_low)
     high = silu(high * jnp.where(lower, scale_front, scale_back) * gain_high)
-    turned = rolled(high)
-    one = [front, jnp.where(lower, high, 0.0), jnp.where(lower, 0.0, turned)]
-    two = [back, jnp.where(lower, turned, 0.0), jnp.where(lower, 0.0, high)]
+    one, two = [], []
+    for front, back, high in zip(shifted(front), shifted(back), shifted(high)):
+        turned = rolled(high)
+        one += [front, jnp.where(lower, high, 0.0), jnp.where(lower, 0.0, turned)]
+        two += [back, jnp.where(lower, turned, 0.0), jnp.where(lower, 0.0, high)]
     return [jnp.concatenate([part.astype(jnp.bfloat16) for part in row], axis=-1) for row in (one, two)]
 
 
@@ -122,7 +132,9 @@
     values = silu(hidden * inverse * gain)
     rest = jnp.zeros(values.shape[:-1] + (LANES // 2,), jnp.float32)
     high = jnp.concatenate([values[..., LANES:], rest], axis=-1)
-    parts = [values[..., :LANES], high, rolled(high)]
+    parts = []
+    for low, high in zip(shifted(values[..., :LANES]), shifted(high)):
+        parts += [low, high, rolled(high)]
     return jnp.concatenate([part.astype(jnp.bfloat16) for part in parts], axis=-1)
 
 
@@ -137,34 +149,26 @@
 def convolved_part(operand, weights_ref, bias_ref, frame, frames, rows):
     width = operand.shape[2]
     channels = weights_ref.shape[-1]
-    taps = [(a, i) for a in range(TAPS) for i in range(TAPS)]
-    groups = [taps[start:start + 2] for start in range(0, len(taps), 2)]
+    taps = [(a, i, j) for a in range(TAPS) for i in range(TAPS) for j in range(TAPS)]
+    lefts, rights = [], []
 
     def window(tap, part):
-        a, i = tap
-        value = operand[frame + a:frame + a + frames, i:i + rows, :, part * LANES:(part + 1) * LANES]
+        a, i, j = tap
+        lane = (3 * j + part) * LANES
+        value = operand[frame + a:frame + a + frames, i:i + rows, :, lane:lane + LANES]
         return value.reshape(frames * rows * width, LANES)
 
-    pieces = []
-    for group in groups:
-        pieces += [window(tap, 0) for tap in group]
+    for start in range(0, len(taps), 2):
+        group = taps[start:start + 2]
+        lefts += [window(tap, 0) for tap in group]
         high = window(group[0], 1)
-        pieces.append(high + window(group[1], 2) if len(group) > 1 else high)
-    left = jnp.concatenate(pieces, axis=-1)
-    products = []
-    for j in range(TAPS):
-        rights = []
-        for group in groups:
-            held = [weights_ref[a, i, j] for a, i in group]
-            rights += [weight[:LANES] for weight in held] + [weight[LANES:] for weight in held]
-        rights.append(jnp.zeros((left.shape[1] - sum(r.shape[0] for r in rights), channels), jnp.bfloat16))
-        product = jnp.dot(left, jnp.concatenate(rights, axis=0), preferred_element_type=jnp.float32)
-        products.append(product.reshape(frames * rows, width, channels))
-    column = lax.broadcasted_iota(jnp.int32, (1, width, 1), 1)
-    before = jnp.where(column == 0, 0.0, pltpu.roll(products[0], 1, 1))
-    after = jnp.where(column == width - 1, 0.0, pltpu.roll(products[2], width - 1, 1))
-    result = products[1] + before + after + bias_ref[...].reshape(1, 1, channels)
-    return result.reshape(frames, rows, width, channels)
+        lefts.append(high + window(group[1], 2) if len(group) > 1 else high)
+        held = [weights_ref[a, i, j] for a, i, j in group]
+        rights += [weight[:LANES] for weight in held] + [weight[LANES:] for weight in held]
+    left = jnp.concatenate(lefts, axis=-1)
+    rights.append(jnp.zeros((left.shape[1] - sum(r.shape[0] for r in rights), channels), jnp.bfloat16))
+    result = jnp.dot(left, jnp.concatenate(rights, axis=0), preferred_element_type=jnp.float32)
+    return (result + bias_ref[...]).reshape(frames, rows, width, channels)
 
 
 def halves(core, mine, other):
@@ -311,12 +315,25 @@
         target[:, pl.ds(2 * (1 - core), inner_rows - 2)] = source[...]
 
 
+def place_kernel(keep_ref, got_ref, result_ref, arrived):
+    core, half = lax.axis_index("wa"), keep_ref.shape[1]
+    copies = [
+        pltpu.make_async_copy(keep_ref, result_ref.at[:, pl.ds(half * core, half)], arrived.at[0]),
+        pltpu.make_async_copy(got_ref, result_ref.at[:, pl.ds(half * (1 - core), half)], arrived.at[1]),
+    ]
+    for copy in copies:
+        copy.start()
+    for copy in copies:
+        copy.wait()
+
+
 def shards(features, frame_counts, gain_first, conv_first, bias_first, gain_second, conv_second, bias_second):
     frames, rows, side, channels = features.shape
     pairs, half = rows // 2, rows // 2
     held = half // 2 + 1
     tall, cores, blocks = lax.axis_size("ha"), lax.axis_size("wa"), lax.axis_size("tchunk")
     packed, width, tiles = 3 * LANES, 2 * side, CACHE * held
+    deep = TAPS * packed
     bf16 = jnp.bfloat16
     vmem = pl.BlockSpec(memory_space=pltpu.VMEM)
     limit = pltpu.CompilerParams(vmem_limit_bytes=20 * 2**20)
@@ -391,12 +408,12 @@
     near, inner, keep, send = pl.pallas_call(
         middle_kernel,
         out_shape=(
-            shape(frames + CACHE, 2, width, packed), shape(frames + 2, half, width, packed),
+            shape(frames + CACHE, 2, width, deep), shape(frames + 2, half, width, deep),
             shape(frames, half - 2, side, channels), shape(frames, half - 2, side, channels),
         ),
         in_specs=[vmem] * 11,
         out_specs=(vmem,) * 4,
-        scratch_shapes=[pltpu.VMEM((frames + CACHE, half + 2, width, packed), bf16)],
+        scratch_shapes=[pltpu.VMEM((frames + CACHE, half + 2, width, deep), bf16)],
         compiler_params=limit,
         cost_estimate=cost(work * ((frames + 2) * half + frames * (half - 2)), 8 * 2**20),
     )(marks, tail_mine, tail_other, mine, other, *weights)
@@ -406,15 +423,21 @@
         in_specs=[vmem] * 16,
         out_specs=(vmem, vmem),
         scratch_shapes=[
-            pltpu.VMEM((frames + CACHE, 4, width, packed), bf16),
-            pltpu.VMEM((frames + 2, 4, width, packed), bf16),
+            pltpu.VMEM((frames + CACHE, 4, width, deep), bf16),
+            pltpu.VMEM((frames + 2, 4, width, deep), bf16),
         ],
         compiler_params=limit,
         cost_estimate=cost(work * 2 * (2 * frames + 2), 8 * 2**20),
     )(marks, tail_mine, mine, other, tail_edge, own_edge, near, inner, keep, send, *weights)
     got = lax.ppermute(send, "wa", swap)
-    upper, lower = halves(lax.axis_index("wa"), keep, got)
-    return jnp.concatenate([upper, lower], axis=1)
+    return pl.pallas_call(
+        place_kernel,
+        out_shape=shape(*features.shape),
+        in_specs=[vmem, vmem],
+        out_specs=pl.BlockSpec(memory_space=pltpu.HBM),
+        scratch_shapes=[pltpu.SemaphoreType.DMA((2,))],
+        compiler_params=limit,
+    )(keep, got)
 
 
 def solution(mesh):

time: 20.4 us -> 21.6 us (1.059)
  Pallas kernels: 5.72 us -> 7.65 us
  other arithmetic: 0.77 us -> 0 us
    ppermute x1, starting transfers between devices: 1.38 us -> 4.51 us  [shards(): tail_other = lax.ppermute(tail_theirs, axes, crossed)]
    ppermute x1, starting transfers between devices: 4.41 us -> 1.29 us  [shards(): tail_mine = lax.ppermute(tail, axes, straight)]
    pallas_call x1, Pallas kernels: 2.97 us -> 3.84 us  [shards(): pl.pallas_call(middle_kernel, out_shape=(shape(frames + CACHE, 2, width,...]
    concatenate x1 -> x0, other arithmetic: 0.75 us -> none  [shards(): return jnp.concatenate([upper, lower], axis=1)]
    ppermute x1, waiting for transfers between devices: 0.74 us -> 0.01 us  [shards(): tail_other = lax.ppermute(tail_theirs, axes, crossed)]
    pallas_call x0 -> x1, Pallas kernels: none -> 0.71 us  [shards(): pl.pallas_call(place_kernel, out_shape=shape(*features.shape), in_specs=[...]
    ppermute x1, waiting for transfers between devices: 0.01 us -> 0.64 us  [shards(): tail_mine = lax.ppermute(tail, axes, straight)]
    pallas_call x1, Pallas kernels: 2.56 us -> 2.92 us  [shards(): pl.pallas_call(outer_kernel, out_shape=(shape(frames, half, side, channel...]
  transfers between devices with their start and end apart: 6 -> 6, of which waited for: 2 -> 2; matrix products, arithmetic and copies ran while one was open for 0% -> 0% of each run, Pallas kernels for 15% -> 18%
where the time goes in v2:
time: 21.6 us; the launch traced here: 21.4 us
  starting transfers between devices  10.8 us (50%)
  Pallas kernels  7.65 us (35%)
  waiting for transfers between devices  1.64 us (8%)
  between operations  0.84 us (4%)
  local copies, waits for them, and re-layouts  0.5 us (2%)
    ppermute x1, starting transfers between devices, shards(): tail_other = lax.ppermute(tail_theirs, axes, crossed)  4.51 us
    pallas_call x1, Pallas kernels, shards(): pl.pallas_call(middle_kernel, out_shape=(shape(frames + CACHE, 2, width,...  3.84 us
    pallas_call x1, Pallas kernels, shards(): pl.pallas_call(outer_kernel, out_shape=(shape(frames, half, side, channel...  2.92 us
    ppermute x1, starting transfers between devices, shards(): got = lax.ppermute(send, 'wa', swap)  2.9 us
    ppermute x1, starting transfers between devices, shards(): tail_mine = lax.ppermute(tail, axes, straight)  1.29 us
    ppermute x1, waiting for transfers between devices, shards(): got = lax.ppermute(send, 'wa', swap)  0.99 us
    ppermute x1, starting transfers between devices, shards(): own_edge = lax.ppermute(own_edge, axes, across)  0.8 us
    ppermute x1, starting transfers between devices, shards(): tail_edge = lax.ppermute(tail_edge, axes, diagonal)  0.8 us
  transfers between devices with their start and end apart: 6, of which 2 were waited for; matrix products, arithmetic and copies ran while one was open for 0% of the time, Pallas kernels for 18%

profile of v2, /device:TPU:0, one launch (start us, length us, event | category | flops | bytes accessed | tf_op | source)
XLA Modules:
  0.0 21.4 jit_solution(14967686870781830710)
XLA Ops:
  0.0 0.0 copy-start.2
  0.7 0.3 %copy-done.2 = bf16[8,8,8,192]{3,2,1,0:T(8,128)(2,1)S(1)} copy-done((bf16[8,8,8,192]{3,2,1,0:T(8,128)(2,1)S(1)}, bf16[8,8,8,192]{3,2,1,0:T(8,128)(2,1)}, u32[]{:S(2)}) %copy-start.2) | copy-done | bytes 196632
  1.0 0.1 shard_map.83
  1.1 0.5 %collective-permute-start.1 = (bf16[36,8,384]{2,1,0:T(8,128)(2,1)S(1)}, bf16[36,8,384]{2,1,0:T(8,128)(2,1)S(1)}, u32[]{:S(2)}, u32[]{:S(2)}) collective-permute-start(bf16[36,8,384]{2,1,0:T(8,128)(2,1)S(1)} %get-tuple-element.24), channel_id=1, source_target_pairs={{0,1},{1,0},{2,3},{3,2},{4,5},{5,4},{6,7},{7,6},{8,9},{9,8},{10,11... | collective-permute-start | bytes 663560 | tf_op jit(solution)/shard_map/ppermute | solution.py:392
  1.6 4.5 %collective-permute-start.4 = (bf16[12,8,384]{2,1,0:T(8,128)(2,1)S(1)}, bf16[12,8,384]{2,1,0:T(8,128)(2,1)S(1)}, u32[]{:S(2)}, u32[]{:S(2)}) collective-permute-start(bf16[12,8,384]{2,1,0:T(8,128)(2,1)S(1)} %slice.3), channel_id=1, source_target_pairs={{0,9},{1,8},{2,11},{3,10},{4,13},{5,12},{6,15},{7,14},{16,25},{17,... | collective-permute-start | bytes 221192 | tf_op jit(solution)/shard_map/ppermute | solution.py:391
  6.2 1.3 %collective-permute-start = (bf16[13,8,384]{2,1,0:T(8,128)(2,1)S(1)}, bf16[13,8,384]{2,1,0:T(8,128)(2,1)S(1)}, u32[]{:S(2)}, u32[]{:S(2)}) collective-permute-start(bf16[13,8,384]{2,1,0:T(8,128)(2,1)S(1)} %get-tuple-element.22.tail_ref), channel_id=1, source_target_pairs={{0,8},{1,9},{2,10},{3,11},{4,12},{5,13},{6,14},{7,15},{16,24},{17,... | collective-permute-start | bytes 239624 | tf_op jit(solution)/shard_map/ppermute | solution.py:390
  7.5 0.0 collective-permute-done.1.other_ref
  7.5 0.0 copy-start
  7.5 0.0 copy-start.1
  7.5 0.0 copy-start.3
  7.5 0.0 copy-start.4
  7.5 0.0 copy-start.5
  7.5 0.0 copy-start.6
  7.6 0.8 %collective-permute-start.2 = (bf16[2,4,8,384]{3,2,1,0:T(8,128)(2,1)S(1)}, bf16[2,4,8,384]{3,2,1,0:T(8,128)(2,1)S(1)}, u32[]{:S(2)}, u32[]{:S(2)}) collective-permute-start(bf16[2,4,8,384]{3,2,1,0:T(8,128)(2,1)S(1)} %get-tuple-element.25), channel_id=1, source_target_pairs={{1,10},{2,9},{3,12},{4,11},{5,14},{6,13},{17,26},{18,25},{19,28},{... | collective-permute-start | bytes 147464 | tf_op jit(solution)/shard_map/ppermute | solution.py:402
  8.4 0.8 %collective-permute-start.3 = (bf16[2,8,8,384]{3,2,1,0:T(8,128)(2,1)S(1)}, bf16[2,8,8,384]{3,2,1,0:T(8,128)(2,1)S(1)}, u32[]{:S(2)}, u32[]{:S(2)}) collective-permute-start(bf16[2,8,8,384]{3,2,1,0:T(8,128)(2,1)S(1)} %get-tuple-element.26), channel_id=1, source_target_pairs={{1,2},{2,1},{9,10},{10,9},{3,4},{4,3},{11,12},{12,11},{5,6},{6,5},... | collective-permute-start | bytes 294920 | tf_op jit(solution)/shard_map/ppermute | solution.py:401
  9.2 0.0 collective-permute-done.4.tail_other_ref
  9.2 0.6 %collective-permute-done.tail_mine_ref = bf16[13,8,384]{2,1,0:T(8,128)(2,1)S(1)} collective-permute-done((bf16[13,8,384]{2,1,0:T(8,128)(2,1)S(1)}, bf16[13,8,384]{2,1,0:T(8,128)(2,1)S(1)}, u32[]{:S(2)}, u32[]{:S(2)}) %collective-permute-start) | collective-permute-done | bytes 79904 | tf_op jit(solution)/shard_map/ppermute | solution.py:390
  9.9 0.0 copy-done
  9.9 0.2 copy-done.1
  10.0 0.0 copy-done.3
  10.0 0.0 copy-done.4
  10.0 0.0 copy-done.5
  10.0 0.0 copy-done.6
  10.1 3.8 %shard_map.85 = (bf16[12,2,16,1152]{3,2,1,0:T(8,128)(2,1)S(1)}, bf16[10,4,16,1152]{3,2,1,0:T(8,128)(2,1)S(1)}, bf16[8,2,8,192]{3,2,1,0:T(8,128)(2,1)S(1)}, bf16[8,2,8,192]{3,2,1,0:T(8,128)(2,1)S(1)}) custom-call(bf16[8,384]{1,0:T(8,128)(2,1)S(1)} %get-tuple-element.21.marks_ref, bf16[13,8,384]{2,1,0:T(8,128)(2,1)S(1)} %collective-permute-done.tail_mine_ref, ...), custom_call_target="tpu_custom_call" | custom-call | flops 1783627776 | bytes 8388608 | tf_op jit(solution)/shard_map/pallas_call | solution.py:408
  13.9 0.0 collective-permute-done.2.tail_edge_ref
  13.9 0.0 collective-permute-done.3.own_edge_ref
  13.9 2.9 %shard_map.86 = (bf16[8,4,8,192]{3,2,1,0:T(8,128)(2,1)S(1)}, bf16[8,4,8,192]{3,2,1,0:T(8,128)(2,1)S(1)}) custom-call(bf16[8,384]{1,0:T(8,128)(2,1)S(1)} %get-tuple-element.21.marks_ref, bf16[13,8,384]{2,1,0:T(8,128)(2,1)S(1)} %collective-permute-done.tail_mine_ref, bf16[8,3,8,384]{3,2,1,0:T(8,128)(2,1)S(1)} %get-tuple-element.23.mine_ref, ...), custom_call_target="tpu_custom_call" | custom-call | flops 1146617856 | bytes 8388608 | tf_op jit(solution)/shard_map/pallas_call | solution.py:420
  16.8 2.9 %collective-permute-start.5 = (bf16[8,4,8,192]{3,2,1,0:T(8,128)(2,1)S(1)}, bf16[8,4,8,192]{3,2,1,0:T(8,128)(2,1)S(1)}, u32[]{:S(2)}, u32[]{:S(2)}) collective-permute-start(bf16[8,4,8,192]{3,2,1,0:T(8,128)(2,1)S(1)} %get-tuple-element.32), channel_id=1, source_target_pairs={{0,1},{1,0},{2,3},{3,2},{4,5},{5,4},{6,7},{7,6},{8,9},{9,8},{10,11... | collective-permute-start | bytes 294920 | tf_op jit(solution)/shard_map/ppermute | solution.py:432
  19.7 1.0 %collective-permute-done.5.got_ref = bf16[8,4,8,192]{3,2,1,0:T(8,128)(2,1)S(1)} collective-permute-done((bf16[8,4,8,192]{3,2,1,0:T(8,128)(2,1)S(1)}, bf16[8,4,8,192]{3,2,1,0:T(8,128)(2,1)S(1)}, u32[]{:S(2)}, u32[]{:S(2)}) %collective-permute-start.5) | collective-permute-done | bytes 98336 | tf_op jit(solution)/shard_map/ppermute | solution.py:432
  20.7 0.7 %shard_map.87 = bf16[8,8,8,192]{3,2,1,0:T(8,128)(2,1)} custom-call(bf16[8,4,8,192]{3,2,1,0:T(8,128)(2,1)S(1)} %get-tuple-element.31.keep_ref, bf16[8,4,8,192]{3,2,1,0:T(8,128)(2,1)S(1)} %collective-permute-done.5.got_ref), custom_call_target="tpu_custom_call" | custom-call | tf_op jit(solution)/shard_map/pallas_call | solution.py:433
  (3 shorter events, 0.0 us)
Async XLA Ops:
  0.0 1.0 %copy-start.2 = (bf16[8,8,8,192]{3,2,1,0:T(8,128)(2,1)S(1)}, bf16[8,8,8,192]{3,2,1,0:T(8,128)(2,1)}, u32[]{:S(2)}) copy-start(bf16[8,8,8,192]{3,2,1,0:T(8,128)(2,1)} %raw.1) | copy-start | bytes 589828
  1.1 6.4 %collective-permute-start.1 = (bf16[36,8,384]{2,1,0:T(8,128)(2,1)S(1)}, bf16[36,8,384]{2,1,0:T(8,128)(2,1)S(1)}, u32[]{:S(2)}, u32[]{:S(2)}) collective-permute-start(bf16[36,8,384]{2,1,0:T(8,128)(2,1)S(1)} %get-tuple-element.24), channel_id=1, source_target_pairs={{0,1},{1,0},{2,3},{3,2},{4,5},{5,4},{6,7},{7,6},{8,9},{9,8},{10,11... | collective-permute-start | bytes 663560 | tf_op jit(solution)/shard_map/ppermute | solution.py:392
  1.6 7.5 %collective-permute-start.4 = (bf16[12,8,384]{2,1,0:T(8,128)(2,1)S(1)}, bf16[12,8,384]{2,1,0:T(8,128)(2,1)S(1)}, u32[]{:S(2)}, u32[]{:S(2)}) collective-permute-start(bf16[12,8,384]{2,1,0:T(8,128)(2,1)S(1)} %slice.3), channel_id=1, source_target_pairs={{0,9},{1,8},{2,11},{3,10},{4,13},{5,12},{6,15},{7,14},{16,25},{17,... | collective-permute-start | bytes 221192 | tf_op jit(solution)/shard_map/ppermute | solution.py:391
  6.2 3.7 %collective-permute-start = (bf16[13,8,384]{2,1,0:T(8,128)(2,1)S(1)}, bf16[13,8,384]{2,1,0:T(8,128)(2,1)S(1)}, u32[]{:S(2)}, u32[]{:S(2)}) collective-permute-start(bf16[13,8,384]{2,1,0:T(8,128)(2,1)S(1)} %get-tuple-element.22.tail_ref), channel_id=1, source_target_pairs={{0,8},{1,9},{2,10},{3,11},{4,12},{5,13},{6,14},{7,15},{16,24},{17,... | collective-permute-start | bytes 239624 | tf_op jit(solution)/shard_map/ppermute | solution.py:390
  7.5 2.4 %copy-start = (bf16[3,3,3,192,192]{4,3,2,1,0:T(8,128)(2,1)S(1)}, bf16[3,3,3,192,192]{4,3,2,1,0:T(8,128)(2,1)}, u32[]{:S(2)}) copy-start(bf16[3,3,3,192,192]{4,3,2,1,0:T(8,128)(2,1)} %w1_ref.3) | copy-start | bytes 5971972
  7.5 2.5 %copy-start.1 = (bf16[3,3,3,192,192]{4,3,2,1,0:T(8,128)(2,1)S(1)}, bf16[3,3,3,192,192]{4,3,2,1,0:T(8,128)(2,1)}, u32[]{:S(2)}) copy-start(bf16[3,3,3,192,192]{4,3,2,1,0:T(8,128)(2,1)} %w2_ref.3) | copy-start | bytes 5971972
  7.5 2.5 %copy-start.3 = (f32[192]{0:T(256)S(1)}, f32[192]{0:T(256)}, u32[]{:S(2)}) copy-start(f32[192]{0:T(256)} %param.10) | copy-start | bytes 2308
  7.5 2.5 %copy-start.4 = (f32[192]{0:T(256)S(1)}, f32[192]{0:T(256)}, u32[]{:S(2)}) copy-start(f32[192]{0:T(256)} %param.12) | copy-start | bytes 2308
  7.5 2.5 %copy-start.5 = (f32[192]{0:T(256)S(1)}, f32[192]{0:T(256)}, u32[]{:S(2)}) copy-start(f32[192]{0:T(256)} %param.13) | copy-start | bytes 2308
  7.5 2.5 %copy-start.6 = (f32[192]{0:T(256)S(1)}, f32[192]{0:T(256)}, u32[]{:S(2)}) copy-start(f32[192]{0:T(256)} %param.15) | copy-start | bytes 2308
  7.6 6.3 %collective-permute-start.2 = (bf16[2,4,8,384]{3,2,1,0:T(8,128)(2,1)S(1)}, bf16[2,4,8,384]{3,2,1,0:T(8,128)(2,1)S(1)}, u32[]{:S(2)}, u32[]{:S(2)}) collective-permute-start(bf16[2,4,8,384]{3,2,1,0:T(8,128)(2,1)S(1)} %get-tuple-element.25), channel_id=1, source_target_pairs={{1,10},{2,9},{3,12},{4,11},{5,14},{6,13},{17,26},{18,25},{19,28},{... | collective-permute-start | bytes 147464 | tf_op jit(solution)/shard_map/ppermute | solution.py:402
  8.4 5.5 %collective-permute-start.3 = (bf16[2,8,8,384]{3,2,1,0:T(8,128)(2,1)S(1)}, bf16[2,8,8,384]{3,2,1,0:T(8,128)(2,1)S(1)}, u32[]{:S(2)}, u32[]{:S(2)}) collective-permute-start(bf16[2,8,8,384]{3,2,1,0:T(8,128)(2,1)S(1)} %get-tuple-element.26), channel_id=1, source_target_pairs={{1,2},{2,1},{9,10},{10,9},{3,4},{4,3},{11,12},{12,11},{5,6},{6,5},... | collective-permute-start | bytes 294920 | tf_op jit(solution)/shard_map/ppermute | solution.py:401
  16.8 3.9 %collective-permute-start.5 = (bf16[8,4,8,192]{3,2,1,0:T(8,128)(2,1)S(1)}, bf16[8,4,8,192]{3,2,1,0:T(8,128)(2,1)S(1)}, u32[]{:S(2)}, u32[]{:S(2)}) collective-permute-start(bf16[8,4,8,192]{3,2,1,0:T(8,128)(2,1)S(1)} %get-tuple-element.32), channel_id=1, source_target_pairs={{0,1},{1,0},{2,3},{3,2},{4,5},{5,4},{6,7},{7,6},{8,9},{9,8},{10,11... | collective-permute-start | bytes 294920 | tf_op jit(solution)/shard_map/ppermute | solution.py:432

commit v3 on v1

--- a/solution.py
+++ b/solution.py
@@ -9,7 +9,7 @@
 CACHE = 4
 TAPS = 3
 LANES = 128
-PRODUCT = 192
+PRODUCT = 160
 
 
 def slots_kernel(slots_ref):
@@ -112,7 +112,7 @@
     turned = rolled(high)
     one = [front, jnp.where(lower, high, 0.0), jnp.where(lower, 0.0, turned)]
     two = [back, jnp.where(lower, turned, 0.0), jnp.where(lower, 0.0, high)]
-    return [jnp.concatenate([part.astype(jnp.bfloat16) for part in row], axis=-1) for row in (one, two)]
+    return [[part.astype(jnp.bfloat16) for part in row] for row in (one, two)]
 
 
 def second_rows(hidden, flag, gain_ref, channels):
@@ -123,11 +123,11 @@
     rest = jnp.zeros(values.shape[:-1] + (LANES // 2,), jnp.float32)
     high = jnp.concatenate([values[..., LANES:], rest], axis=-1)
     parts = [values[..., :LANES], high, rolled(high)]
-    return jnp.concatenate([part.astype(jnp.bfloat16) for part in parts], axis=-1)
+    return jnp.stack([part.astype(jnp.bfloat16) for part in parts])
 
 
 def convolved(operand, weights_ref, bias_ref, frame, frames, rows, then):
-    products = -(-frames * rows * operand.shape[2] // PRODUCT)
+    products = -(-frames * rows * operand.shape[3] // PRODUCT)
     step = -(-frames // products)
     for start in range(0, frames, step):
         count = min(step, frames - start)
@@ -135,14 +135,14 @@
 
 
 def convolved_part(operand, weights_ref, bias_ref, frame, frames, rows):
-    width = operand.shape[2]
+    width = operand.shape[3]
     channels = weights_ref.shape[-1]
     taps = [(a, i) for a in range(TAPS) for i in range(TAPS)]
     groups = [taps[start:start + 2] for start in range(0, len(taps), 2)]
 
     def window(tap, part):
         a, i = tap
-        value = operand[frame + a:frame + a + frames, i:i + rows, :, part * LANES:(part + 1) * LANES]
+        value = operand[part, frame + a:frame + a + frames, i:i + rows]
         return value.reshape(frames * rows * width, LANES)
 
     pieces = []
@@ -180,9 +180,10 @@
     left, right = halves(lax.axis_index("wa"), mine, other)
     frames, pairs = mine.shape[:2]
     upper, lower = first_rows(left, right, gain_ref, channels)
-    for pair in range(pairs):
-        operand[frame:frame + frames, 2 * pair] = upper[:, pair]
-        operand[frame:frame + frames, 2 * pair + 1] = lower[:, pair]
+    for part in range(len(upper)):
+        for pair in range(pairs):
+            operand[part, frame:frame + frames, 2 * pair] = upper[part][:, pair]
+            operand[part, frame:frame + frames, 2 * pair + 1] = lower[part][:, pair]
 
 
 def border_kernel(tail_ref, mine_ref, other_ref, tail_edge_ref, own_edge_ref):
@@ -237,7 +238,7 @@
     def hide(first, count, flags):
         def then(start, part, hidden):
             flag = jnp.concatenate(flags[start:start + part], axis=0)
-            inner_ref[first + start:first + start + part] = second_rows(hidden, flag, gain2_ref, channels)
+            inner_ref[:, first + start:first + start + part] = second_rows(hidden, flag, gain2_ref, channels)
 
         convolved(operand, w1_ref, bias1_ref, first, count, rows - 2, then)
 
@@ -250,11 +251,11 @@
 
     @pl.when(jnp.logical_not(earlier))
     def _():
-        operand[0:CACHE] = jnp.zeros((CACHE,) + operand.shape[1:], operand.dtype)
-        inner_ref[0:2] = jnp.zeros((2,) + inner_ref.shape[1:], inner_ref.dtype)
+        operand[:, 0:CACHE] = jnp.zeros(operand.shape[:1] + (CACHE,) + operand.shape[2:], operand.dtype)
+        inner_ref[:, 0:2] = jnp.zeros(inner_ref.shape[:1] + (2,) + inner_ref.shape[2:], inner_ref.dtype)
 
     fill_rows(operand, CACHE, mine_ref[...], unpacked(other_ref, tiles, frames), gain1_ref, channels)
-    near_ref[...] = operand[:, pl.ds((rows - 2) * core, 2)]
+    near_ref[...] = operand[:, :, pl.ds((rows - 2) * core, 2)]
     hide(2, frames, live)
 
     def put(ref):
@@ -275,26 +276,27 @@
 ):
     core, place = lax.axis_index("wa"), lax.axis_index("ha")
     frames, pairs = mine_ref.shape[:2]
-    inner_rows = inner_ref.shape[1]
+    inner_rows = inner_ref.shape[2]
     channels = w1_ref.shape[-1]
     outward, inward = pl.ds(2 * core, 2), pl.ds(2 * (1 - core), 2)
 
     for start, ref in ((0, tail_edge_ref), (CACHE, own_edge_ref)):
         left, right = halves(core, ref[1], ref[0])
         upper, lower = first_rows(left[:, None], right[:, None], gain1_ref, channels)
-        strip[start:start + ref.shape[1], pl.ds(2 * core, 1)] = upper
-        strip[start:start + ref.shape[1], pl.ds(2 * core + 1, 1)] = lower
-    strip[:, inward] = near_ref[...]
+        for part in range(len(upper)):
+            strip[part, start:start + ref.shape[1], pl.ds(2 * core, 1)] = upper[part]
+            strip[part, start:start + ref.shape[1], pl.ds(2 * core + 1, 1)] = lower[part]
+    strip[:, :, inward] = near_ref[...]
     inside = jnp.where(core == 0, place > 0, place < lax.axis_size("ha") - 1)
     row = lax.broadcasted_iota(jnp.int32, (1, 2, 1, 1), 1)
     row_flag = jnp.where((row == core) & jnp.logical_not(inside), 0.0, 1.0)
     live = frame_flags(marks_ref[...], range(frames))
     flags = frame_flags(tail_mine_ref[CACHE * pairs], range(CACHE - 2, CACHE)) + live
-    operand[:, inward] = inner_ref[:, pl.ds((inner_rows - 2) * core, 2)]
+    operand[:, :, inward] = inner_ref[:, :, pl.ds((inner_rows - 2) * core, 2)]
 
     def hide(start, part, hidden):
         flag = jnp.concatenate(flags[start:start + part], axis=0) * row_flag
-        operand[start:start + part, outward] = second_rows(hidden, flag, gain2_ref, channels)
+        operand[:, start:start + part, outward] = second_rows(hidden, flag, gain2_ref, channels)
 
     convolved(strip, w1_ref, bias1_ref, 0, frames + 2, 2, hide)
 
@@ -309,6 +311,18 @@
     convolved(operand, w2_ref, bias2_ref, 0, frames, 2, then)
     for source, target in ((keep_mid_ref, keep_ref), (send_mid_ref, send_ref)):
         target[:, pl.ds(2 * (1 - core), inner_rows - 2)] = source[...]
+
+
+def place_kernel(keep_ref, got_ref, result_ref, arrived):
+    core, half = lax.axis_index("wa"), keep_ref.shape[1]
+    copies = [
+        pltpu.make_async_copy(keep_ref, result_ref.at[:, pl.ds(half * core, half)], arrived.at[0]),
+        pltpu.make_async_copy(got_ref, result_ref.at[:, pl.ds(half * (1 - core), half)], arrived.at[1]),
+    ]
+    for copy in copies:
+        copy.start()
+    for copy in copies:
+        copy.wait()
 
 
 def shards(features, frame_counts, gain_first, conv_first, bias_first, gain_second, conv_second, bias_second):
@@ -391,12 +405,12 @@
     near, inner, keep, send = pl.pallas_call(
         middle_kernel,
         out_shape=(
-            shape(frames + CACHE, 2, width, packed), shape(frames + 2, half, width, packed),
+            shape(3, frames + CACHE, 2, width, LANES), shape(3, frames + 2, half, width, LANES),
             shape(frames, half - 2, side, channels), shape(frames, half - 2, side, channels),
         ),
         in_specs=[vmem] * 11,
         out_specs=(vmem,) * 4,
-        scratch_shapes=[pltpu.VMEM((frames + CACHE, half + 2, width, packed), bf16)],
+        scratch_shapes=[pltpu.VMEM((3, frames + CACHE, half + 2, width, LANES), bf16)],
         compiler_params=limit,
         cost_estimate=cost(work * ((frames + 2) * half + frames * (half - 2)), 8 * 2**20),
     )(marks, tail_mine, tail_other, mine, other, *weights)
@@ -406,15 +420,21 @@
         in_specs=[vmem] * 16,
         out_specs=(vmem, vmem),
         scratch_shapes=[
-            pltpu.VMEM((frames + CACHE, 4, width, packed), bf16),
-            pltpu.VMEM((frames + 2, 4, width, packed), bf16),
+            pltpu.VMEM((3, frames + CACHE, 4, width, LANES), bf16),
+            pltpu.VMEM((3, frames + 2, 4, width, LANES), bf16),
         ],
         compiler_params=limit,
         cost_estimate=cost(work * 2 * (2 * frames + 2), 8 * 2**20),
     )(marks, tail_mine, mine, other, tail_edge, own_edge, near, inner, keep, send, *weights)
     got = lax.ppermute(send, "wa", swap)
-    upper, lower = halves(lax.axis_index("wa"), keep, got)
-    return jnp.concatenate([upper, lower], axis=1)
+    return pl.pallas_call(
+        place_kernel,
+        out_shape=shape(*features.shape),
+        in_specs=[vmem, vmem],
+        out_specs=pl.BlockSpec(memory_space=pltpu.HBM),
+        scratch_shapes=[pltpu.SemaphoreType.DMA((2,))],
+        compiler_params=limit,
+    )(keep, got)
 
 
 def solution(mesh):

time: 20.4 us -> 20.6 us (level)
  other arithmetic: 0.77 us -> 0 us
  Pallas kernels: 5.72 us -> 6.39 us
    ppermute x1, starting transfers between devices: 1.38 us -> 4.51 us  [shards(): tail_other = lax.ppermute(tail_theirs, axes, crossed)]
    ppermute x1, starting transfers between devices: 4.41 us -> 1.29 us  [shards(): tail_mine = lax.ppermute(tail, axes, straight)]
    concatenate x1 -> x0, other arithmetic: 0.75 us -> none  [shards(): return jnp.concatenate([upper, lower], axis=1)]
    ppermute x1, waiting for transfers between devices: 0.74 us -> 0.01 us  [shards(): tail_other = lax.ppermute(tail_theirs, axes, crossed)]
    pallas_call x1 -> x2, Pallas kernels: 2.97 us -> 3.68 us  [the longest x1 2.97 us: shards(): pl.pallas_call(middle_kernel, out_shape=(shape(3, frames + CACHE, 2, widt...]
    ppermute x1, waiting for transfers between devices: 0.01 us -> 0.64 us  [shards(): tail_mine = lax.ppermute(tail, axes, straight)]
    ppermute x1, starting transfers between devices: 2.87 us -> 3.12 us  [shards(): got = lax.ppermute(send, 'wa', swap)]
where the time goes in v3:
time: 20.6 us; the launch traced here: 20.4 us
  starting transfers between devices  11 us (53%)
  Pallas kernels  6.39 us (31%)
  waiting for transfers between devices  1.64 us (8%)
  between operations  0.84 us (4%)
  local copies, waits for them, and re-layouts  0.5 us (2%)
    ppermute x1, starting transfers between devices, shards(): tail_other = lax.ppermute(tail_theirs, axes, crossed)  4.51 us
    ppermute x1, starting transfers between devices, shards(): got = lax.ppermute(send, 'wa', swap)  3.12 us
    pallas_call x1, Pallas kernels, shards(): pl.pallas_call(middle_kernel, out_shape=(shape(3, frames + CACHE, 2, widt...  2.97 us
    pallas_call x1, Pallas kernels, shards(): pl.pallas_call(outer_kernel, out_shape=(shape(frames, half, side, channel...  2.52 us
    ppermute x1, starting transfers between devices, shards(): tail_mine = lax.ppermute(tail, axes, straight)  1.29 us
    ppermute x1, waiting for transfers between devices, shards(): got = lax.ppermute(send, 'wa', swap)  0.99 us
    ppermute x1, starting transfers between devices, shards(): own_edge = lax.ppermute(own_edge, axes, across)  0.8 us
    ppermute x1, starting transfers between devices, shards(): tail_edge = lax.ppermute(tail_edge, axes, diagonal)  0.8 us
  transfers between devices with their start and end apart: 6, of which 2 were waited for; matrix products, arithmetic and copies ran while one was open for 0% of the time, Pallas kernels for 15%

profile of v3, /device:TPU:0, one launch (start us, length us, event | category | flops | bytes accessed | tf_op | source)
XLA Modules:
  0.0 20.4 jit_solution(4971413227237047267)
XLA Ops:
  0.0 0.0 copy-start.2
  0.7 0.3 %copy-done.2 = bf16[8,8,8,192]{3,2,1,0:T(8,128)(2,1)S(1)} copy-done((bf16[8,8,8,192]{3,2,1,0:T(8,128)(2,1)S(1)}, bf16[8,8,8,192]{3,2,1,0:T(8,128)(2,1)}, u32[]{:S(2)}) %copy-start.2) | copy-done | bytes 196632
  1.0 0.1 shard_map.83
  1.1 0.5 %collective-permute-start.1 = (bf16[36,8,384]{2,1,0:T(8,128)(2,1)S(1)}, bf16[36,8,384]{2,1,0:T(8,128)(2,1)S(1)}, u32[]{:S(2)}, u32[]{:S(2)}) collective-permute-start(bf16[36,8,384]{2,1,0:T(8,128)(2,1)S(1)} %get-tuple-element.24), channel_id=1, source_target_pairs={{0,1},{1,0},{2,3},{3,2},{4,5},{5,4},{6,7},{7,6},{8,9},{9,8},{10,11... | collective-permute-start | bytes 663560 | tf_op jit(solution)/shard_map/ppermute | solution.py:389
  1.6 4.5 %collective-permute-start.4 = (bf16[12,8,384]{2,1,0:T(8,128)(2,1)S(1)}, bf16[12,8,384]{2,1,0:T(8,128)(2,1)S(1)}, u32[]{:S(2)}, u32[]{:S(2)}) collective-permute-start(bf16[12,8,384]{2,1,0:T(8,128)(2,1)S(1)} %slice.3), channel_id=1, source_target_pairs={{0,9},{1,8},{2,11},{3,10},{4,13},{5,12},{6,15},{7,14},{16,25},{17,... | collective-permute-start | bytes 221192 | tf_op jit(solution)/shard_map/ppermute | solution.py:388
  6.2 1.3 %collective-permute-start = (bf16[13,8,384]{2,1,0:T(8,128)(2,1)S(1)}, bf16[13,8,384]{2,1,0:T(8,128)(2,1)S(1)}, u32[]{:S(2)}, u32[]{:S(2)}) collective-permute-start(bf16[13,8,384]{2,1,0:T(8,128)(2,1)S(1)} %get-tuple-element.22.tail_ref), channel_id=1, source_target_pairs={{0,8},{1,9},{2,10},{3,11},{4,12},{5,13},{6,14},{7,15},{16,24},{17,... | collective-permute-start | bytes 239624 | tf_op jit(solution)/shard_map/ppermute | solution.py:387
  7.5 0.0 collective-permute-done.1.other_ref
  7.5 0.0 copy-start
  7.5 0.0 copy-start.1
  7.5 0.0 copy-start.3
  7.5 0.0 copy-start.4
  7.5 0.0 copy-start.5
  7.5 0.0 copy-start.6
  7.6 0.8 %collective-permute-start.2 = (bf16[2,4,8,384]{3,2,1,0:T(8,128)(2,1)S(1)}, bf16[2,4,8,384]{3,2,1,0:T(8,128)(2,1)S(1)}, u32[]{:S(2)}, u32[]{:S(2)}) collective-permute-start(bf16[2,4,8,384]{3,2,1,0:T(8,128)(2,1)S(1)} %get-tuple-element.25), channel_id=1, source_target_pairs={{1,10},{2,9},{3,12},{4,11},{5,14},{6,13},{17,26},{18,25},{19,28},{... | collective-permute-start | bytes 147464 | tf_op jit(solution)/shard_map/ppermute | solution.py:399
  8.4 0.8 %collective-permute-start.3 = (bf16[2,8,8,384]{3,2,1,0:T(8,128)(2,1)S(1)}, bf16[2,8,8,384]{3,2,1,0:T(8,128)(2,1)S(1)}, u32[]{:S(2)}, u32[]{:S(2)}) collective-permute-start(bf16[2,8,8,384]{3,2,1,0:T(8,128)(2,1)S(1)} %get-tuple-element.26), channel_id=1, source_target_pairs={{1,2},{2,1},{9,10},{10,9},{3,4},{4,3},{11,12},{12,11},{5,6},{6,5},... | collective-permute-start | bytes 294920 | tf_op jit(solution)/shard_map/ppermute | solution.py:398
  9.2 0.0 collective-permute-done.4.tail_other_ref
  9.2 0.6 %collective-permute-done.tail_mine_ref = bf16[13,8,384]{2,1,0:T(8,128)(2,1)S(1)} collective-permute-done((bf16[13,8,384]{2,1,0:T(8,128)(2,1)S(1)}, bf16[13,8,384]{2,1,0:T(8,128)(2,1)S(1)}, u32[]{:S(2)}, u32[]{:S(2)}) %collective-permute-start) | collective-permute-done | bytes 79904 | tf_op jit(solution)/shard_map/ppermute | solution.py:387
  9.8 0.0 copy-done
  9.9 0.2 copy-done.1
  10.0 0.0 copy-done.3
  10.0 0.0 copy-done.4
  10.0 0.0 copy-done.5
  10.0 0.0 copy-done.6
  10.1 3.0 %shard_map.85 = (bf16[3,12,2,16,128]{4,3,2,1,0:T(8,128)(2,1)S(1)}, bf16[3,10,4,16,128]{4,3,2,1,0:T(8,128)(2,1)S(1)}, bf16[8,2,8,192]{3,2,1,0:T(8,128)(2,1)S(1)}, bf16[8,2,8,192]{3,2,1,0:T(8,128)(2,1)S(1)}) custom-call(bf16[8,384]{1,0:T(8,128)(2,1)S(1)} %get-tuple-element.21.marks_ref, bf16[13,8,384]{2,1,0:T(8,128)(2,1)S(1)} %collective-permute-done.tail_mine_ref, ...), custom_call_target="tpu_custom_call" | custom-call | flops 1783627776 | bytes 8388608 | tf_op jit(solution)/shard_map/pallas_call | solution.py:405
  13.0 0.0 collective-permute-done.2.tail_edge_ref
  13.0 0.0 collective-permute-done.3.own_edge_ref
  13.0 2.5 %shard_map.86 = (bf16[8,4,8,192]{3,2,1,0:T(8,128)(2,1)S(1)}, bf16[8,4,8,192]{3,2,1,0:T(8,128)(2,1)S(1)}) custom-call(bf16[8,384]{1,0:T(8,128)(2,1)S(1)} %get-tuple-element.21.marks_ref, bf16[13,8,384]{2,1,0:T(8,128)(2,1)S(1)} %collective-permute-done.tail_mine_ref, bf16[8,3,8,384]{3,2,1,0:T(8,128)(2,1)S(1)} %get-tuple-element.23.mine_ref, ...), custom_call_target="tpu_custom_call" | custom-call | flops 1146617856 | bytes 8388608 | tf_op jit(solution)/shard_map/pallas_call | solution.py:417
  15.6 3.1 %collective-permute-start.5 = (bf16[8,4,8,192]{3,2,1,0:T(8,128)(2,1)S(1)}, bf16[8,4,8,192]{3,2,1,0:T(8,128)(2,1)S(1)}, u32[]{:S(2)}, u32[]{:S(2)}) collective-permute-start(bf16[8,4,8,192]{3,2,1,0:T(8,128)(2,1)S(1)} %get-tuple-element.32), channel_id=1, source_target_pairs={{0,1},{1,0},{2,3},{3,2},{4,5},{5,4},{6,7},{7,6},{8,9},{9,8},{10,11... | collective-permute-start | bytes 294920 | tf_op jit(solution)/shard_map/ppermute | solution.py:429
  18.7 1.0 %collective-permute-done.5.got_ref = bf16[8,4,8,192]{3,2,1,0:T(8,128)(2,1)S(1)} collective-permute-done((bf16[8,4,8,192]{3,2,1,0:T(8,128)(2,1)S(1)}, bf16[8,4,8,192]{3,2,1,0:T(8,128)(2,1)S(1)}, u32[]{:S(2)}, u32[]{:S(2)}) %collective-permute-start.5) | collective-permute-done | bytes 98336 | tf_op jit(solution)/shard_map/ppermute | solution.py:429
  19.7 0.7 %shard_map.87 = bf16[8,8,8,192]{3,2,1,0:T(8,128)(2,1)} custom-call(bf16[8,4,8,192]{3,2,1,0:T(8,128)(2,1)S(1)} %get-tuple-element.31.keep_ref, bf16[8,4,8,192]{3,2,1,0:T(8,128)(2,1)S(1)} %collective-permute-done.5.got_ref), custom_call_target="tpu_custom_call" | custom-call | tf_op jit(solution)/shard_map/pallas_call | solution.py:430
  (3 shorter events, 0.0 us)
Async XLA Ops:
  0.0 1.0 %copy-start.2 = (bf16[8,8,8,192]{3,2,1,0:T(8,128)(2,1)S(1)}, bf16[8,8,8,192]{3,2,1,0:T(8,128)(2,1)}, u32[]{:S(2)}) copy-start(bf16[8,8,8,192]{3,2,1,0:T(8,128)(2,1)} %raw.1) | copy-start | bytes 589828
  1.1 6.4 %collective-permute-start.1 = (bf16[36,8,384]{2,1,0:T(8,128)(2,1)S(1)}, bf16[36,8,384]{2,1,0:T(8,128)(2,1)S(1)}, u32[]{:S(2)}, u32[]{:S(2)}) collective-permute-start(bf16[36,8,384]{2,1,0:T(8,128)(2,1)S(1)} %get-tuple-element.24), channel_id=1, source_target_pairs={{0,1},{1,0},{2,3},{3,2},{4,5},{5,4},{6,7},{7,6},{8,9},{9,8},{10,11... | collective-permute-start | bytes 663560 | tf_op jit(solution)/shard_map/ppermute | solution.py:389
  1.6 7.5 %collective-permute-start.4 = (bf16[12,8,384]{2,1,0:T(8,128)(2,1)S(1)}, bf16[12,8,384]{2,1,0:T(8,128)(2,1)S(1)}, u32[]{:S(2)}, u32[]{:S(2)}) collective-permute-start(bf16[12,8,384]{2,1,0:T(8,128)(2,1)S(1)} %slice.3), channel_id=1, source_target_pairs={{0,9},{1,8},{2,11},{3,10},{4,13},{5,12},{6,15},{7,14},{16,25},{17,... | collective-permute-start | bytes 221192 | tf_op jit(solution)/shard_map/ppermute | solution.py:388
  6.2 3.7 %collective-permute-start = (bf16[13,8,384]{2,1,0:T(8,128)(2,1)S(1)}, bf16[13,8,384]{2,1,0:T(8,128)(2,1)S(1)}, u32[]{:S(2)}, u32[]{:S(2)}) collective-permute-start(bf16[13,8,384]{2,1,0:T(8,128)(2,1)S(1)} %get-tuple-element.22.tail_ref), channel_id=1, source_target_pairs={{0,8},{1,9},{2,10},{3,11},{4,12},{5,13},{6,14},{7,15},{16,24},{17,... | collective-permute-start | bytes 239624 | tf_op jit(solution)/shard_map/ppermute | solution.py:387
  7.5 2.4 %copy-start = (bf16[3,3,3,192,192]{4,3,2,1,0:T(8,128)(2,1)S(1)}, bf16[3,3,3,192,192]{4,3,2,1,0:T(8,128)(2,1)}, u32[]{:S(2)}) copy-start(bf16[3,3,3,192,192]{4,3,2,1,0:T(8,128)(2,1)} %w1_ref.3) | copy-start | bytes 5971972
  7.5 2.5 %copy-start.1 = (bf16[3,3,3,192,192]{4,3,2,1,0:T(8,128)(2,1)S(1)}, bf16[3,3,3,192,192]{4,3,2,1,0:T(8,128)(2,1)}, u32[]{:S(2)}) copy-start(bf16[3,3,3,192,192]{4,3,2,1,0:T(8,128)(2,1)} %w2_ref.3) | copy-start | bytes 5971972
  7.5 2.5 %copy-start.3 = (f32[192]{0:T(256)S(1)}, f32[192]{0:T(256)}, u32[]{:S(2)}) copy-start(f32[192]{0:T(256)} %param.10) | copy-start | bytes 2308
  7.5 2.5 %copy-start.4 = (f32[192]{0:T(256)S(1)}, f32[192]{0:T(256)}, u32[]{:S(2)}) copy-start(f32[192]{0:T(256)} %param.12) | copy-start | bytes 2308
  7.5 2.5 %copy-start.5 = (f32[192]{0:T(256)S(1)}, f32[192]{0:T(256)}, u32[]{:S(2)}) copy-start(f32[192]{0:T(256)} %param.13) | copy-start | bytes 2308
  7.5 2.5 %copy-start.6 = (f32[192]{0:T(256)S(1)}, f32[192]{0:T(256)}, u32[]{:S(2)}) copy-start(f32[192]{0:T(256)} %param.15) | copy-start | bytes 2308
  7.6 5.4 %collective-permute-start.2 = (bf16[2,4,8,384]{3,2,1,0:T(8,128)(2,1)S(1)}, bf16[2,4,8,384]{3,2,1,0:T(8,128)(2,1)S(1)}, u32[]{:S(2)}, u32[]{:S(2)}) collective-permute-start(bf16[2,4,8,384]{3,2,1,0:T(8,128)(2,1)S(1)} %get-tuple-element.25), channel_id=1, source_target_pairs={{1,10},{2,9},{3,12},{4,11},{5,14},{6,13},{17,26},{18,25},{19,28},{... | collective-permute-start | bytes 147464 | tf_op jit(solution)/shard_map/ppermute | solution.py:399
  8.4 4.7 %collective-permute-start.3 = (bf16[2,8,8,384]{3,2,1,0:T(8,128)(2,1)S(1)}, bf16[2,8,8,384]{3,2,1,0:T(8,128)(2,1)S(1)}, u32[]{:S(2)}, u32[]{:S(2)}) collective-permute-start(bf16[2,8,8,384]{3,2,1,0:T(8,128)(2,1)S(1)} %get-tuple-element.26), channel_id=1, source_target_pairs={{1,2},{2,1},{9,10},{10,9},{3,4},{4,3},{11,12},{12,11},{5,6},{6,5},... | collective-permute-start | bytes 294920 | tf_op jit(solution)/shard_map/ppermute | solution.py:398
  15.6 4.1 %collective-permute-start.5 = (bf16[8,4,8,192]{3,2,1,0:T(8,128)(2,1)S(1)}, bf16[8,4,8,192]{3,2,1,0:T(8,128)(2,1)S(1)}, u32[]{:S(2)}, u32[]{:S(2)}) collective-permute-start(bf16[8,4,8,192]{3,2,1,0:T(8,128)(2,1)S(1)} %get-tuple-element.32), channel_id=1, source_target_pairs={{0,1},{1,0},{2,3},{3,2},{4,5},{5,4},{6,7},{7,6},{8,9},{9,8},{10,11... | collective-permute-start | bytes 294920 | tf_op jit(solution)/shard_map/ppermute | solution.py:429
